TPU v7x, 256 devices: a whole 4x4x8 slice. The times are simulated.
256 devices in a mesh: pa: 32 (over x, y, core), ch: 8 (over z).
Axes of the slice: x: 4, y: 4, z: 8, core: 2. Of those that a mesh axis runs over, the one named last changes fastest.
Arguments:
- basis_prev: float32 [64, 48, 4, 2048], P('pa', None, None, 'ch')
- basis_now: float32 [64, 48, 4, 2048], P('pa', None, None, 'ch')
- beta_prev: float32 [4], replicated, may hold values from 0.3 to 0.9
- propagator: float32 [64, 48, 4], P('pa'), may hold values from 0.3 to 1
- spline: bfloat16 [32, 32, 4, 48, 16], P(None, 'pa'), may hold values from -0.25 to 0.25
- coupling: bfloat16 [3, 2048, 2048], P(None, None, 'ch'), as said below
- edge_offset: int32 [32, 32, 4], replicated, may hold values from 0 to 80
- edge_tile: int32 [32, 32, 4], replicated, may hold values from 0 to 1
- edge_term: int32 [32, 32, 4], replicated, may hold values from 0 to 2
- edge_count: int32 [32, 32], replicated, may hold values from 0 to 4, as said below
Outputs:
- basis_next: float32 [64, 48, 4, 2048], P('pa', None, None, 'ch')
- coefficients: float32 [4, 4], replicated
Inputs may be any that keep to these rules, and one draw needn't show every extreme that they name: `edge_count`: in every draw some target interval has all 4 slots live from every source interval. Each of the 3 coupling matrices is symmetric.
All inputs are finite; a program needn't handle non-finite values.
Results may differ from a plain program's by a relative error of at most 0.006.
Values may be sent and summed in bfloat16 or wider, within the bound.
A program may use at most 64 MiB of HBM per device.

v0:
```python
import jax
import jax.numpy as jnp
from jax import lax
from jax.sharding import PartitionSpec as P

ITERS = 2


epsilon = 1e-06


def inner_sum(left, right):
    return jnp.sum(left * right, axis=(0, 1, 3))


def body(
    basis_prev,
    basis_now,
    beta_prev,
    propagator,
    spline,
    coupling,
    edge_offset,
    edge_tile,
    edge_term,
    edge_count,
):
    p_local, q_count, energies, ch_local = basis_now.shape
    term_count, channels, _ = coupling.shape
    intervals = edge_count.shape[0]
    slot_count = edge_offset.shape[2]
    support = spline.shape[-1]
    cell_count = float(p_local * intervals * q_count * channels)
    feature_cols = energies * ch_local
    position = lax.axis_index("pa")
    offset_list = lax.dynamic_index_in_dim(edge_offset, position, 0, keepdims=False)
    tile_list = lax.dynamic_index_in_dim(edge_tile, position, 1, keepdims=False)
    term_list = lax.dynamic_index_in_dim(edge_term, position, 1, keepdims=False)
    count_list = lax.dynamic_index_in_dim(edge_count, position, 1, keepdims=False)
    live_slots = jnp.arange(slot_count, dtype=jnp.int32)[None, :] < count_list[:, None]
    term_hit = (
        term_list[:, :, None, None] == jnp.arange(term_count, dtype=jnp.int32)[None, None, :, None]
    )
    tile_hit = (
        tile_list[:, :, None, None] == jnp.arange(p_local, dtype=jnp.int32)[None, None, None, :]
    )
    selector = (term_hit & tile_hit & live_slots[:, :, None, None]).astype(jnp.bfloat16)
    spline_matrix = jnp.einsum("slkt,slqj->ktqslj", selector, spline[:, 0])
    spline_matrix = spline_matrix.reshape(
        term_count * p_local * q_count, intervals * slot_count * support
    )
    support_index = (
        offset_list[:, :, None] + jnp.arange(support, dtype=jnp.int32)[None, None, :]
    ).reshape(-1)
    basis_old, basis_cur, beta_old = (basis_prev, basis_now, beta_prev)
    coefficients = []
    for iteration in range(ITERS):
        flat_field = basis_cur.astype(jnp.bfloat16).reshape(p_local * q_count, feature_cols)
        outgoing = jnp.take(flat_field, support_index, axis=0).reshape(
            intervals, slot_count, support, feature_cols
        )
        incoming = lax.all_to_all(outgoing, "pa", split_axis=0, concat_axis=0, tiled=True)
        interpolated = jnp.dot(
            spline_matrix,
            incoming.reshape(intervals * slot_count * support, feature_cols),
            preferred_element_type=jnp.float32,
        )
        coupled = interpolated.astype(jnp.bfloat16).reshape(
            term_count, p_local * q_count * energies, ch_local
        )
        result = jnp.einsum(
            "krc,kcd->rd",
            lax.all_gather(coupled, "ch", axis=2, tiled=True),
            coupling,
            preferred_element_type=jnp.float32,
        )
        applied = basis_cur - propagator[..., None] * result.reshape(
            p_local, q_count, energies, ch_local
        )
        alpha_now = lax.psum(inner_sum(basis_cur, applied), ("pa", "ch")) / cell_count
        residual = applied - alpha_now[:, None] * basis_cur - beta_old[:, None] * basis_old
        squares = lax.psum(inner_sum(residual, residual), ("pa", "ch"))
        beta_now = jnp.sqrt(squares / cell_count + epsilon)
        basis_old, basis_cur, beta_old = (basis_cur, residual / beta_now[:, None], beta_now)
        coefficients.append(alpha_now)
        coefficients.append(beta_now)
    return (basis_cur, jnp.stack(coefficients))


def solution(mesh):
    placed = (
        P("pa", None, None, "ch"),
        P("pa", None, None, "ch"),
        P(),
        P("pa", None, None),
        P(None, "pa", None, None, None),
        P(None, None, "ch"),
        P(),
        P(),
        P(),
        P(),
    )
    return jax.shard_map(
        body,
        mesh=mesh,
        in_specs=placed,
        out_specs=(P("pa", None, None, "ch"), P()),
        check_vma=False,
    )
```

profile of v0, /device:TPU:1, one launch (start us, length us, event | category | flops | bytes accessed | tf_op | source)
XLA Modules:
  0.0 625.5 jit_solution(3025512683278088736)
XLA Ops:
  7.2 0.8 dynamic-slice_bitcast_fusion
  8.0 0.1 copy.24
  8.1 0.1 iota_add_fusion
  8.2 0.1 add.53
  8.3 1.1 convert_element_type.13
  9.4 9.7 %gather_fusion = bf16[2048,1024]{1,0:T(8,128)(2,1)} fusion(bf16[96,1024]{1,0:T(8,128)(2,1)S(1)} %bitcast.40, s32[2048]{0:T(1024)S(1)} %fusion), kind=kCustom, calls=%fused_computation.clone | custom fusion | bytes 8396800 | tf_op jit(solution)/shard_map/jit(_take)/gather | solution.py:59
  19.1 3.8 broadcast_select_fusion.1
  22.9 8.8 %all-to-all-start = ((bf16[32,4,16,1024]{3,2,1,0:T(8,128)(2,1)}), bf16[32,4,16,1024]{3,2,1,0:T(8,128)(2,1)}, u32[]{:S(2)}, u32[]{:S(2)}) async-start(bf16[32,4,16,1024]{3,2,1,0:T(8,128)(2,1)} %bitcast.41), calls=%async_computation | async-start | bytes 8388608 | tf_op jit(solution)/shard_map/all_to_all | solution.py:62
  31.8 0.1 constant_dynamic-slice_fusion
  31.9 0.1 copy.22
  32.0 0.1 copy.20
  32.1 0.1 copy.21
  32.2 0.1 copy.23
  32.3 0.2 dynamic-slice_reduce_fusion
  32.6 0.1 iota_compare_fusion.1
  32.7 0.1 iota_compare_fusion
  32.8 0.3 and_convert_fusion
  33.2 5.7 multiply_bitcast_fusion
  38.9 6.6 %reshape.94 = bf16[288,2048]{0,1:T(8,128)(2,1)} reshape(bf16[3,2,48,32,4,16]{2,1,0,5,4,3:T(2,128)(2,1)} %multiply_bitcast_fusion) | data formatting | bytes 2359296 | tf_op jit(solution)/shard_map/reshape | solution.py:49
  45.5 38.5 %all-to-all-done = bf16[32,4,16,1024]{3,2,1,0:T(8,128)(2,1)} async-done(((bf16[32,4,16,1024]{3,2,1,0:T(8,128)(2,1)}), bf16[32,4,16,1024]{3,2,1,0:T(8,128)(2,1)}, u32[]{:S(2)}, u32[]{:S(2)}) %all-to-all-start) | async-done | bytes 4194336 | tf_op jit(solution)/shard_map/all_to_all | solution.py:62
  84.0 4.9 convolution_convert_fusion.1
  88.9 2.2 reshape.98
  91.2 0.7 copy.19
  91.9 65.3 %all-gather.3.cloned.1.call-done = bf16[3,384,2048]{2,1,0:T(8,128)(2,1)} async-done(((bf16[3,384,256]{2,1,0:T(8,128)(2,1)}), bf16[3,384,2048]{2,1,0:T(8,128)(2,1)}) %all-gather.3.cloned.1.call-update) | async-done | bytes 4718608 | tf_op jit(solution)/shard_map/all_gather | solution.py:73
  157.1 4.5 convolution_bitcast_fusion.1
  161.6 1.8 reshape.99
  163.5 1.9 multiply_reduce_fusion.3
  165.4 78.0 %psum.28 = f32[4]{0:T(128)} all-reduce(f32[4]{0:T(128)} %multiply_reduce_fusion.3), channel_id=1, replica_groups=mesh['pa'=32,'ch'=8] {'pa','ch'}, use_global_device_ids=true, to_apply=%region_1.3 | all-reduce | flops 4 | bytes 32 | tf_op jit(solution)/shard_map/psum | solution.py:80
  243.3 1.2 fusion.1
  244.6 2.8 multiply_reduce_fusion.2
  247.3 73.7 %psum.29 = f32[4]{0:T(128)S(1)} all-reduce(f32[4]{0:T(128)} %get-tuple-element.5), channel_id=1, replica_groups=mesh['pa'=32,'ch'=8] {'pa','ch'}, use_global_device_ids=true, to_apply=%region_3.5 | all-reduce | flops 4 | bytes 32 | tf_op jit(solution)/shard_map/psum | solution.py:82
  321.0 0.5 fusion.3
  321.6 1.1 fusion.5
  322.7 9.7 %gather_fusion.1 = bf16[2048,1024]{1,0:T(8,128)(2,1)} fusion(bf16[96,1024]{1,0:T(8,128)(2,1)S(1)} %bitcast.39, s32[2048]{0:T(1024)S(1)} %fusion), kind=kCustom, calls=%fused_computation.1.clone | custom fusion | bytes 8396800 | tf_op jit(solution)/shard_map/jit(_take)/gather | solution.py:59
  332.4 2.5 broadcast_select_fusion
  334.9 55.6 %all_to_all.10 = bf16[32,4,16,1024]{3,2,1,0:T(8,128)(2,1)S(1)} all-to-all(bf16[32,4,16,1024]{3,2,1,0:T(8,128)(2,1)S(1)} %bitcast.42), channel_id=1, replica_groups=mesh['pa'=32,'ch'=8] {'pa'}, dimensions={0} | all-to-all | bytes 8388608 | tf_op jit(solution)/shard_map/all_to_all | solution.py:62
  390.5 2.3 convolution_convert_fusion
  392.8 2.2 reshape.103
  395.0 58.2 %all-gather.5.cloned.1.call-done = bf16[3,384,2048]{2,1,0:T(8,128)(2,1)} async-done(((bf16[3,384,256]{2,1,0:T(8,128)(2,1)}), bf16[3,384,2048]{2,1,0:T(8,128)(2,1)}) %all-gather.5.cloned.1.call-update) | async-done | bytes 4718608 | tf_op jit(solution)/shard_map/all_gather | solution.py:73
  453.2 4.5 convolution_bitcast_fusion
  457.7 1.8 reshape.104
  459.6 1.5 multiply_reduce_fusion.1
  461.1 77.9 %psum.30 = f32[4]{0:T(128)S(1)} all-reduce(f32[4]{0:T(128)S(1)} %multiply_reduce_fusion.1), channel_id=1, replica_groups=mesh['pa'=32,'ch'=8] {'pa','ch'}, use_global_device_ids=true, to_apply=%region_5.7 | all-reduce | flops 4 | bytes 32 | tf_op jit(solution)/shard_map/psum | solution.py:80
  539.0 0.6 fusion.2
  539.5 2.3 multiply_reduce_fusion
  541.9 73.7 %psum.31 = f32[4]{0:T(128)S(1)} all-reduce(f32[4]{0:T(128)S(1)} %get-tuple-element.3), channel_id=1, replica_groups=mesh['pa'=32,'ch'=8] {'pa','ch'}, use_global_device_ids=true, to_apply=%region_7.9 | all-reduce | flops 4 | bytes 32 | tf_op jit(solution)/shard_map/psum | solution.py:82
  615.5 1.9 broadcast_divide_fusion
  617.4 1.3 pad_maximum_fusion
  (30 shorter events, 0.3 us)
Async XLA Ops:
  7.2 150.0 %copy-start = (bf16[3,2048,256]{2,1,0:T(8,128)(2,1)S(1)}, bf16[3,2048,256]{2,1,0:T(8,128)(2,1)}, u32[]{:S(2)}) copy-start(bf16[3,2048,256]{2,1,0:T(8,128)(2,1)} %param.17) | copy-start | bytes 9437188
  22.9 8.8 %copy-start.4 = (s32[32,32,4]{1,2,0:T(4,128)S(1)}, s32[32,32,4]{1,2,0:T(4,128)}, u32[]{:S(2)}) copy-start(s32[32,32,4]{1,2,0:T(4,128)} %param.19) | copy-start | bytes 49156
  22.9 8.9 %copy-start.5 = (s32[32,32,4]{1,2,0:T(4,128)S(1)}, s32[32,32,4]{1,2,0:T(4,128)}, u32[]{:S(2)}) copy-start(s32[32,32,4]{1,2,0:T(4,128)} %param.20) | copy-start | bytes 49156
  22.9 9.4 %copy-start.6 = (s32[32,32]{1,0:T(8,128)S(1)}, s32[32,32]{1,0:T(8,128)}, u32[]{:S(2)}) copy-start(s32[32,32]{1,0:T(8,128)} %param.21) | copy-start | bytes 12292
  22.9 61.0 %all-to-all-start = ((bf16[32,4,16,1024]{3,2,1,0:T(8,128)(2,1)}), bf16[32,4,16,1024]{3,2,1,0:T(8,128)(2,1)}, u32[]{:S(2)}, u32[]{:S(2)}) async-start(bf16[32,4,16,1024]{3,2,1,0:T(8,128)(2,1)} %bitcast.41), calls=%async_computation | async-start | bytes 8388608 | tf_op jit(solution)/shard_map/all_to_all | solution.py:62
  31.7 125.4 %all-gather.3.cloned.1.call-start = ((), (), s32[]{:S(2)}) async-start(), calls=%async_computation.2 | async-start | bytes 5308416 | tf_op jit(solution)/shard_map/all_gather | solution.py:73
  83.9 7.2 %copy-start.7 = (f32[2,48,4]{1,2,0:T(4,128)S(1)}, f32[2,48,4]{1,2,0:T(4,128)}, u32[]{:S(2)}) copy-start(f32[2,48,4]{1,2,0:T(4,128)} %param.15) | copy-start | bytes 4612
  91.1 362.1 %all-gather.5.cloned.1.call-start = ((), (), s32[]{:S(2)}) async-start(), calls=%async_computation.3 | async-start | bytes 5308416 | tf_op jit(solution)/shard_map/all_gather | solution.py:73
  91.9 71.6 %copy-start.1 = (f32[2,48,4,256]{3,2,1,0:T(4,128)S(1)}, f32[2,48,4,256]{3,2,1,0:T(4,128)}, u32[]{:S(2)}) copy-start(f32[2,48,4,256]{3,2,1,0:T(4,128)} %param.13) | copy-start | bytes 1179652
  91.9 152.7 %copy-start.8 = (f32[4]{0:T(128)S(1)}, f32[4]{0:T(128)}, u32[]{:S(2)}) copy-start(f32[4]{0:T(128)} %param.14) | copy-start | bytes 52
  334.9 55.6 %copy-start.3 = (bf16[288,2048]{0,1:T(8,128)(2,1)S(1)}, bf16[288,2048]{0,1:T(8,128)(2,1)}, u32[]{:S(2)}) copy-start(bf16[288,2048]{0,1:T(8,128)(2,1)} %reshape.94) | copy-start | bytes 3538948
  395.0 144.5 %copy-start.2 = (f32[2,48,4,256]{3,2,1,0:T(4,128)S(1)}, f32[2,48,4,256]{3,2,1,0:T(4,128)}, u32[]{:S(2)}) copy-start(f32[2,48,4,256]{3,2,1,0:T(4,128)} %param.13) | copy-start | bytes 1179652
  395.0 222.4 %copy-start.9 = (f32[1,4]{1,0:T(1,128)S(1)}, f32[1,4]{1,0:T(1,128)}, u32[]{:S(2)}) copy-start(f32[1,4]{1,0:T(1,128)} %get-tuple-element.7) | copy-start | bytes 52
Sparse Core Ops, SparseCore 0:
  91.2 65.8 all-gather.2
  395.1 58.0 all-gather.4
where the time goes:
time: 627 us; the launch traced here: 626 us
  blocking collectives  359 us (57%)
  waiting for transfers between devices  162 us (26%)
  local copies, waits for them, and re-layouts  36.5 us (6%)
  other arithmetic  29 us (5%)
  matrix products  16.1 us (3%)
  between operations  14.2 us (2%)
  starting transfers between devices  8.87 us (1%)
    psum x2, blocking collectives, body(): lax.psum(inner_sum(basis_cur, applied), ('pa', 'ch')) / cell_count  156 us
    psum x2, blocking collectives, body(): squares = lax.psum(inner_sum(residual, residual), ('pa', 'ch'))  147 us
    all_gather x2, waiting for transfers between devices, body(): lax.all_gather(coupled, 'ch', axis=2, tiled=True)  123 us
    all_to_all x1, blocking collectives, body(): lax.all_to_all(outgoing, 'pa', split_axis=0, concat_axis=0, tiled=True)  55.6 us
    all_to_all x1, waiting for transfers between devices, body(): lax.all_to_all(outgoing, 'pa', split_axis=0, concat_axis=0, tiled=True)  38.5 us
    gather x2, local copies, waits for them, and re-layouts, body(): jnp.take(flat_field, support_index, axis=0)  19.3 us
  transfers between devices with their start and end apart: 3, of which 3 were waited for; matrix products, arithmetic and copies ran while one was open for 2% of the time, Pallas kernels for 0%

commit v1 on v0

v1 whole, which is shorter than its diff:
```python
import jax
import jax.numpy as jnp
from jax import lax
from jax.experimental import pallas as pl
from jax.experimental.pallas import tpu as pltpu
from jax.sharding import PartitionSpec as P

MESH = pl.DeviceIdType.MESH
EPS = 1e-06
ROWS = 96
HALF = 48
CH = 256
CELLS = 6291456.0


def shifted(position):
    c = position % 2
    y = (position // 2) % 4
    return position // 8, (y - c + 4) % 4, c


def place(x, yp, c):
    return (x * 4 + (yp + c) % 4) * 2 + c


def energy_of(t, g):
    return (t % 2) * 2 + 1 - (t // 2 + g) % 2


def kernel(
    q1_in,
    q0_in,
    beta_in,
    prop_in,
    sp_in,
    meta_in,
    cpl,
    out,
    coef,
    xs,
    spg,
    dmat,
    xg,
    acc,
    u2,
    pbuf,
    rs_s,
    rs_r,
    q1g,
    q0g,
    pg,
    y1g,
    sg,
    q2g,
    s2g,
    fin_q,
    fin_s,
    redv,
    red_a,
    redt,
    red_b,
    coefg,
    sem_x,
    sem_in,
    sem_ag,
    sem_rs,
    sem_ra,
    sem_rb,
    sem_fin,
):
    pa = lax.axis_index("pa")
    z = lax.axis_index("ch")
    X, yp, c = shifted(pa)
    g = yp // 2
    th = yp % 2
    tme = th * 2 + c
    a = 1 - (th + g) % 2
    e = c * 2 + a
    j = X * 2 + g
    f32 = jnp.float32
    bf16 = jnp.bfloat16

    def member(t):
        return (place(X, 2 * g + t // 2, t % 2), z)

    def peer(jj):
        gg = jj % 2
        return (place(jj // 2, 2 * gg + (gg + 1 - a) % 2, c), z)

    others = [(tme + d) % 4 for d in range(1, 4)]
    peers = [(j + d) % 8 for d in range(1, 8)]
    zs = [(z + d) % 8 for d in range(1, 8)]

    barrier = pltpu.get_barrier_semaphore()
    friends = [member(t) for t in others] + [peer(p) for p in peers] + [(pa, q) for q in zs]
    for d in friends:
        pl.semaphore_signal(barrier, inc=1, device_id=d, device_id_type=MESH)
    pl.semaphore_wait(barrier, len(friends))

    def remote(src, dst, send, recv, device):
        return pltpu.make_async_remote_copy(
            src_ref=src, dst_ref=dst, send_sem=send, recv_sem=recv, device_id=device, device_id_type=MESH
        )

    def x_copy(d, slot):
        t = others[d]
        return remote(xs.at[d], xg.at[0, slot, j], sem_x.at[0, d], sem_x.at[1, slot], member(t))

    def in_copy(kind, d, slot):
        t = others[d]
        em = energy_of(t, g)
        src = (sp_in, q1_in.at[em], q0_in.at[em], prop_in.at[em])[kind]
        dst = (spg, q1g, q0g, pg)[kind].at[slot]
        return remote(src, dst, sem_in.at[0, kind, d], sem_in.at[1, kind, slot], member(t))

    for d in range(3):
        xs[d] = q1_in[energy_of(others[d], g)].astype(bf16)
        x_copy(d, tme).start()
    for d in range(3):
        in_copy(0, d, tme).start()
    xg[0, tme, j] = q1_in[e].astype(bf16)
    spg[tme] = sp_in[...]
    q1g[tme] = q1_in[e]
    q0g[tme] = q0_in[e]
    pg[tme] = prop_in[e]

    xr, xl, xo = (X + 1) % 4, (X + 3) % 4, (X + 2) % 4
    dev_r, dev_l = peer(xr * 2 + g), peer(xl * 2 + g)
    dev_p = peer(X * 2 + 1 - g)

    def ag_ref(it, t, slot, part):
        if part is None:
            return xg.at[it, t, slot]
        return xg.at[it, t, slot, pl.ds(part * HALF, HALF)]

    def ag_send(it, t, k):
        slot, part, dev = (
            (j, None, dev_r),
            (j, None, dev_l),
            (xl * 2 + g, 0, dev_r),
            (xr * 2 + g, 1, dev_l),
            (j, None, dev_p),
            (xl * 2 + g, None, dev_p),
            (xr * 2 + g, None, dev_p),
            (xo * 2 + g, 0, dev_p),
            (xo * 2 + g, 1, dev_p),
        )[k]
        ref = ag_ref(it, t, slot, part)
        return remote(ref, ref, sem_ag.at[it, 0, t, k], sem_ag.at[it, 1, t, k], dev)

    def ag_recv(it, t, k):
        h = 1 - g
        slot, part = (
            (xl * 2 + g, None),
            (xr * 2 + g, None),
            (xo * 2 + g, 0),
            (xo * 2 + g, 1),
            (X * 2 + h, None),
            (xl * 2 + h, None),
            (xr * 2 + h, None),
            (xo * 2 + h, 0),
            (xo * 2 + h, 1),
        )[k]
        ref = ag_ref(it, t, slot, part)
        remote(ref, ref, sem_ag.at[it, 0, t, k], sem_ag.at[it, 1, t, k], dev_p).wait_recv()

    def ag_first(it, t):
        for k in (0, 1, 4):
            ag_send(it, t, k).start()

    def ag_second(it, t):
        ag_recv(it, t, 0)
        ag_send(it, t, 2).start()
        ag_send(it, t, 5).start()
        ag_recv(it, t, 1)
        ag_send(it, t, 3).start()
        ag_send(it, t, 6).start()

    def ag_third(it, t):
        for k in (2, 3):
            ag_recv(it, t, k)
            ag_send(it, t, k + 5).start()

    def ag_last(it, t):
        for k in (4, 5, 6, 7, 8):
            ag_recv(it, t, k)

    row_ids = lax.broadcasted_iota(jnp.int32, (4 * ROWS, CH), 0)

    def build(tt):
        def one(ts, carry):
            for half in range(2):
                b = ts * 2 + half
                meta = meta_in[tt, b]
                key = lax.shift_right_logical(meta, 10)
                row = meta & 1023
                tile = spg[tt, b]
                parts = []
                for kt in range(6):
                    mask = jnp.where(key == kt, 1.0, 0.0).astype(bf16)
                    parts.append(tile * mask)
                weights = jnp.concatenate(parts, axis=0)
                hot = jnp.where(row_ids == row, 1.0, 0.0).astype(bf16)
                block = lax.dot_general(weights, hot, (((1,), (1,)), ((), ())), preferred_element_type=f32)
                dmat[ts, tt, :, half * 384 : half * 384 + 384] = block.astype(bf16)
            return carry

        lax.fori_loop(0, 4, one, 0)

    def spline_step(it, ts, first, last):
        def one(tt, carry):
            field = xg[it, ts].reshape(8 * ROWS, CH)
            part = jnp.dot(dmat[ts, tt], field, preferred_element_type=f32)
            if not first:
                part = acc[tt] + part
            if last:
                for k in range(3):
                    u2[tt, :, k * CH : (k + 1) * CH] = part[k * ROWS : (k + 1) * ROWS].astype(bf16)
            else:
                acc[tt] = part
            return carry

        lax.fori_loop(0, 4, one, 0)

    def couple(r):
        dest = (z + r) % 8
        rows = pl.ds(pl.multiple_of(dest * CH, CH), CH)
        total = None
        for k in range(3):
            left = u2[:, :, k * CH : (k + 1) * CH].reshape(4 * ROWS, CH)
            part = lax.dot_general(left, cpl[k, rows, :], (((1,), (1,)), ((), ())), preferred_element_type=f32)
            total = part if total is None else total + part
        pbuf[r] = total.reshape(4, ROWS, CH)

    z_dev = ((pa, (z + 1) % 8), (pa, (z + 7) % 8))

    def rs_copy(it, way, step, t):
        if step == 0:
            src = rs_s.at[it, way, 0, t, pl.ds(way * HALF, HALF)]
            dst = rs_r.at[it, way, 0, t, pl.ds(way * HALF, HALF)]
        else:
            src = rs_s.at[it, way, step, t]
            dst = rs_r.at[it, way, step, t]
        return remote(src, dst, sem_rs.at[it, 0, way, step, t], sem_rs.at[it, 1, way, step, t], z_dev[way])

    def rs_begin(it):
        couple(4)

        def one(t, carry):
            for way in range(2):
                lo = way * HALF
                rs_s[it, way, 0, t, lo : lo + HALF] = pbuf[4, t, lo : lo + HALF].astype(bf16)
                rs_copy(it, way, 0, t).start()
            return carry

        lax.fori_loop(0, 4, one, 0)

    def rs_step(it, step):
        rel = (4 - step, 4 + step)
        couple(rel[0])
        couple(rel[1])

        def one(t, carry):
            for way in range(2):
                rs_copy(it, way, step - 1, t).wait_recv()
                if step == 1:
                    lo = way * HALF
                    hi = HALF - lo
                    rs_s[it, way, 1, t, lo : lo + HALF] = (
                        pbuf[rel[way], t, lo : lo + HALF] + rs_r[it, way, 0, t, lo : lo + HALF].astype(f32)
                    ).astype(bf16)
                    rs_s[it, way, 1, t, hi : hi + HALF] = pbuf[rel[way], t, hi : hi + HALF].astype(bf16)
                else:
                    rs_s[it, way, step, t] = (
                        pbuf[rel[way], t] + rs_r[it, way, step - 1, t].astype(f32)
                    ).astype(bf16)
                rs_copy(it, way, step, t).start()
            return carry

        lax.fori_loop(0, 4, one, 0)

    def rs_end(it, t):
        for way in range(2):
            rs_copy(it, way, 3, t).wait_recv()
        return pbuf[0, t] + (rs_r[it, 0, 3, t].astype(f32) + rs_r[it, 1, 3, t].astype(f32))

    def fold(it, row, value):
        line = jnp.sum(value, axis=0, keepdims=True)
        redv[it, row : row + 1, :] += line[:, :128] + line[:, 128:]

    def ra_copy(it, q, slot):
        return remote(redv.at[it], red_a.at[it, slot], sem_ra.at[it, 0, q], sem_ra.at[it, 1, slot], (pa, q))

    def rb_copy(it, p, slot):
        return remote(redt.at[it], red_b.at[it, slot], sem_rb.at[it, 0, p], sem_rb.at[it, 1, slot], peer(p))

    def reduce_first(it):
        red_a[it, z] = redv[it]
        for q in zs:
            ra_copy(it, q, z).start()

    def reduce_second(it):
        for q in zs:
            ra_copy(it, q, q).wait_recv()
        total = red_a[it, 0]
        for i in range(1, 8):
            total = total + red_a[it, i]
        redt[it] = total
        red_b[it, j] = total
        for p in peers:
            rb_copy(it, p, j).start()

    def reduce_last(it):
        for p in peers:
            rb_copy(it, p, p).wait_recv()
        total = red_b[it, 0]
        for i in range(1, 8):
            total = total + red_b[it, i]
        sums = jnp.sum(total, axis=1, keepdims=True)
        qw, ss, sq, qq = sums[0:1], sums[1:2], sums[2:3], sums[3:4]
        alpha = qw / CELLS
        rest = 1.0 - alpha
        squares = ss + 2.0 * rest * sq + rest * rest * qq
        beta = jnp.sqrt(jnp.maximum(squares, 0.0) / CELLS + EPS)
        return alpha, rest, beta

    redv[...] = jnp.zeros_like(redv)
    ag_first(0, tme)
    for d in range(3):
        x_copy(d, others[d]).wait_recv()
        ag_first(0, others[d])
    build(tme)
    order = [tme] + others
    for t in order:
        ag_second(0, t)
    for kind in (1, 2, 3):
        for d in range(3):
            in_copy(kind, d, tme).start()
    for d in range(3):
        in_copy(0, d, others[d]).wait_recv()
        build(others[d])
        if d == 0:
            for t in order:
                ag_third(0, t)
    for t in range(4):
        ag_last(0, t)
        spline_step(0, t, t == 0, t == 3)
    rs_begin(0)
    for step in (1, 2, 3):
        rs_step(0, step)
    couple(0)
    for kind in (1, 2, 3):
        for d in range(3):
            in_copy(kind, d, others[d]).wait_recv()
    beta0 = beta_in[e][0:1, 0:1]

    def first_end(t):
        y = rs_end(0, t)
        y1g[t] = y
        q1 = q1g[t]
        pw = jnp.concatenate([pg[t], pg[t]], axis=1) * y
        s = -pw - beta0 * q0g[t]
        sg[t] = s
        xg[1, t, j] = s.astype(bf16)
        ag_first(1, t)
        fold(0, 0, q1 * (q1 - pw))
        fold(0, 1, s * s)
        fold(0, 2, s * q1)
        fold(0, 3, q1 * q1)

    first_end(0)
    first_end(1)
    ag_second(1, 0)
    first_end(2)
    ag_second(1, 1)
    ag_third(1, 0)
    first_end(3)
    reduce_first(0)

    ag_second(1, 2)
    ag_third(1, 1)
    ag_second(1, 3)
    ag_third(1, 2)
    ag_last(1, 0)
    spline_step(1, 0, True, False)
    reduce_second(0)
    ag_third(1, 3)
    for t in range(1, 4):
        ag_last(1, t)
        spline_step(1, t, False, t == 3)
    rs_begin(1)
    rs_step(1, 1)
    alpha1, rest1, beta1 = reduce_last(0)

    def fin_copy(kind, d, slot):
        t = others[d]
        src = (q2g.at[t], s2g.at[t], coefg.at[e])[kind]
        dst = (fin_q, fin_s, coefg)[kind].at[slot]
        return remote(src, dst, sem_fin.at[0, kind, d], sem_fin.at[1, kind, slot], member(t))

    for t in range(4):
        q2g[t] = (sg[t] + rest1 * q1g[t]) / beta1
    fin_q[e] = q2g[tme]
    for d in range(3):
        fin_copy(0, d, e).start()
    rs_step(1, 2)
    rs_step(1, 3)
    couple(0)
    for t in range(4):
        y = (rs_end(1, t) + rest1 * y1g[t]) / beta1
        q2 = q2g[t]
        pw = jnp.concatenate([pg[t], pg[t]], axis=1) * y
        s = -pw - beta1 * q1g[t]
        s2g[t] = s
        fold(1, 0, q2 * (q2 - pw))
        fold(1, 1, s * s)
        fold(1, 2, s * q2)
        fold(1, 3, q2 * q2)
    reduce_first(1)
    fin_s[e] = s2g[tme]
    for d in range(3):
        fin_copy(1, d, e).start()
    reduce_second(1)
    alpha2, rest2, beta2 = reduce_last(1)
    wide = lambda v: jnp.broadcast_to(v, (1, 128))
    coefg[e] = jnp.concatenate(
        [wide(alpha1), wide(beta1), wide(alpha2), wide(beta2), jnp.zeros((4, 128), f32)], axis=0
    )
    for d in range(3):
        fin_copy(2, d, e).start()
    for kind in range(3):
        for d in range(3):
            fin_copy(kind, d, energy_of(others[d], g)).wait_recv()
    lanes = lax.broadcasted_iota(jnp.int32, (8, 128), 1)
    table = jnp.zeros((8, 128), f32)
    for q in range(4):
        mine = coefg[q]
        table = jnp.where(lanes == q, mine, table)
        rest = 1.0 - mine[2:3, 0:1]
        out[q] = (fin_s[q] + rest * fin_q[q]) / mine[3:4, 0:1]
    coef[...] = table

    for d in range(3):
        x_copy(d, tme).wait_send()
        for kind in range(4):
            in_copy(kind, d, tme).wait_send()
        for kind in range(3):
            fin_copy(kind, d, e).wait_send()
    for it in range(2):

        def drain(t, carry):
            for k in range(9):
                ag_send(it, t, k).wait_send()
            for way in range(2):
                for step in range(4):
                    rs_copy(it, way, step, t).wait_send()
            return carry

        lax.fori_loop(0, 4, drain, 0)
        for q in zs:
            ra_copy(it, q, z).wait_send()
        for p in peers:
            rb_copy(it, p, j).wait_send()


def reorder(values):
    tail = values.shape[1:]
    values = values.reshape((4, 4, 2) + tail)
    values = jnp.stack([values[:, :, 0], jnp.roll(values[:, :, 1], -1, axis=1)], axis=2)
    values = values.reshape((2, 2, 2, 2, 2) + tail)
    rest = tuple(range(5, 5 + len(tail)))
    return values.transpose((3, 4, 0, 1, 2) + rest).reshape((8, 4) + tail)


def body(
    basis_prev,
    basis_now,
    beta_prev,
    propagator,
    spline,
    coupling,
    edge_offset,
    edge_tile,
    edge_term,
    edge_count,
):
    f32 = jnp.float32
    bf16 = jnp.bfloat16
    by_energy = lambda v: v.reshape(ROWS, 4, CH).transpose(1, 0, 2)
    q1 = by_energy(basis_now)
    q0 = by_energy(basis_prev)
    prop = jnp.broadcast_to(propagator.reshape(ROWS, 4).T[:, :, None], (4, ROWS, 128))
    beta = jnp.broadcast_to(beta_prev[:, None, None], (4, 8, 128))
    tiles = reorder(spline[:, 0])
    tiles = tiles.transpose(0, 3, 1, 2, 4).reshape(8, HALF, CH)

    X, yp, _ = shifted(lax.axis_index("pa"))
    targets = jnp.stack([place(X, 2 * (yp // 2) + t // 2, t % 2) for t in range(4)])
    live = jnp.arange(4, dtype=jnp.int32)[None, None, :] < edge_count[:, :, None]
    packed = jnp.where(live, edge_term * 2 + edge_tile, 6) * 1024 + edge_offset
    packed = reorder(jnp.take(packed, targets, axis=1))
    packed = packed.transpose(2, 0, 1, 3)[..., None]
    shift = (
        jnp.arange(4, dtype=jnp.int32)[:, None, None] * ROWS + jnp.arange(16, dtype=jnp.int32)[None, None, :]
    )
    meta = (packed + shift).reshape(4, 8, 1, CH)

    vmem = pl.BlockSpec(memory_space=pltpu.VMEM)
    dma = pltpu.SemaphoreType.DMA
    out, coef = pl.pallas_call(
        kernel,
        out_shape=(
            jax.ShapeDtypeStruct((4, ROWS, CH), f32),
            jax.ShapeDtypeStruct((8, 128), f32),
        ),
        in_specs=[vmem] * 7,
        out_specs=(vmem, vmem),
        scratch_shapes=[
            pltpu.VMEM((3, ROWS, CH), bf16),
            pltpu.VMEM((4, 8, HALF, CH), bf16),
            pltpu.VMEM((4, 4, 288, 768), bf16),
            pltpu.VMEM((2, 4, 8, ROWS, CH), bf16),
            pltpu.VMEM((4, 288, CH), f32),
            pltpu.VMEM((4, ROWS, 768), bf16),
            pltpu.VMEM((8, 4, ROWS, CH), f32),
            pltpu.VMEM((2, 2, 4, 4, ROWS, CH), bf16),
            pltpu.VMEM((2, 2, 4, 4, ROWS, CH), bf16),
            pltpu.VMEM((4, ROWS, CH), f32),
            pltpu.VMEM((4, ROWS, CH), f32),
            pltpu.VMEM((4, ROWS, 128), f32),
            pltpu.VMEM((4, ROWS, CH), f32),
            pltpu.VMEM((4, ROWS, CH), f32),
            pltpu.VMEM((4, ROWS, CH), f32),
            pltpu.VMEM((4, ROWS, CH), f32),
            pltpu.VMEM((4, ROWS, CH), f32),
            pltpu.VMEM((4, ROWS, CH), f32),
            pltpu.VMEM((2, 8, 128), f32),
            pltpu.VMEM((2, 8, 8, 128), f32),
            pltpu.VMEM((2, 8, 128), f32),
            pltpu.VMEM((2, 8, 8, 128), f32),
            pltpu.VMEM((4, 8, 128), f32),
            dma((2, 4)),
            dma((2, 4, 4)),
            dma((2, 2, 4, 9)),
            dma((2, 2, 2, 4, 4)),
            dma((2, 2, 8)),
            dma((2, 2, 8)),
            dma((2, 3, 4)),
        ],
        compiler_params=pltpu.CompilerParams(
            collective_id=0, has_side_effects=True, vmem_limit_bytes=56 * 1024 * 1024
        ),
    )(q1, q0, beta, prop, tiles, meta, coupling)
    basis_next = out.transpose(1, 0, 2).reshape(2, 48, 4, CH)
    return basis_next, coef[:4, :4]


def solution(mesh):
    placed = (
        P("pa", None, None, "ch"),
        P("pa", None, None, "ch"),
        P(),
        P("pa", None, None),
        P(None, "pa", None, None, None),
        P(None, None, "ch"),
        P(),
        P(),
        P(),
        P(),
    )
    return jax.shard_map(
        body,
        mesh=mesh,
        in_specs=placed,
        out_specs=(P("pa", None, None, "ch"), P()),
        check_vma=False,
    )
```

time: 627 us -> 128 us (0.20)
  blocking collectives: 359 us -> 0 us
  waiting for transfers between devices: 162 us -> 0 us
  Pallas kernels: 0 us -> 113 us
  other arithmetic: 29 us -> 1.22 us
  local copies, waits for them, and re-layouts: 36.5 us -> 12.4 us
  matrix products: 16.1 us -> 0 us
  between operations: 14.2 us -> 0.97 us
  starting transfers between devices: 8.87 us -> 0 us
    psum x4 -> x0, blocking collectives: 303 us -> none  [the longest x2 156 us: body(): lax.psum(inner_sum(basis_cur, applied), ('pa', 'ch')) / cell_count]
    all_gather x2 -> x0, waiting for transfers between devices: 123 us -> none  [body(): lax.all_gather(coupled, 'ch', axis=2, tiled=True)]
    pallas_call x0 -> x1, Pallas kernels: none -> 113 us  [body(): pl.pallas_call(kernel, out_shape=(jax.ShapeDtypeStruct((4, ROWS, CH), f32...]
    all_to_all x1 -> x0, blocking collectives: 55.6 us -> none  [body(): lax.all_to_all(outgoing, 'pa', split_axis=0, concat_axis=0, tiled=True)]
    all_to_all x1 -> x0, waiting for transfers between devices: 38.5 us -> none  [body(): lax.all_to_all(outgoing, 'pa', split_axis=0, concat_axis=0, tiled=True)]
    gather x2, local copies, waits for them, and re-layouts: 19.3 us -> 0.68 us  [body(): packed = reorder(jnp.take(packed, targets, axis=1))]
    dot_general x4 -> x0, matrix products: 16.1 us -> none  [the longest x2 8.95 us: body(): jnp.einsum('krc,kcd->rd', lax.all_gather(coupled, 'ch', axis=2, tiled=Tru...]
    reshape x5 -> x2, local copies, waits for them, and re-layouts: 14.7 us -> 0.96 us  [the longest x1 0.87 us: body(): tiles = tiles.transpose(0, 3, 1, 2, 4).reshape(8, HALF, CH)]
  transfers between devices with their start and end apart: 3 -> 0, of which waited for: 3 -> 0; matrix products, arithmetic and copies ran while one was open for 2% -> 0% of each run, Pallas kernels for 0% -> 0%
where the time goes in v1:
time: 128 us; the launch traced here: 127 us
  Pallas kernels  113 us (88%)
  local copies, waits for them, and re-layouts  12.4 us (10%)
    pallas_call x1, Pallas kernels, body(): pl.pallas_call(kernel, out_shape=(jax.ShapeDtypeStruct((4, ROWS, CH), f32...  113 us
    unnamed x18, local copies, waits for them, and re-layouts  7.23 us

profile of v1, /device:TPU:1, one launch (start us, length us, event | category | flops | bytes accessed | tf_op | source)
XLA Modules:
  0.0 127.3 jit_solution(16481160627619543644)
XLA Ops:
  0.6 0.0 copy-start
  0.8 0.1 compare_and_fusion
  0.9 0.1 fusion
  0.9 0.9 copy.50
  1.9 0.9 copy.51
  2.8 0.9 copy.52
  3.7 0.8 copy.49
  4.6 0.6 gather_fusion
  5.2 0.1 copy.53
  5.3 0.1 broadcast_select_fusion
  5.4 0.1 fusion.2
  5.4 0.0 copy-start.1
  5.5 0.1 copy.56
  5.7 0.0 copy-start.2
  5.7 0.2 add.136
  5.9 0.2 add.137
  6.1 0.1 iota_add_fusion
  6.2 0.1 add.142
  6.3 0.6 broadcast_add_fusion.meta_in
  6.9 0.0 copy-done
  6.9 0.0 copy-start.3
  6.9 0.0 copy-start.4
  7.0 0.1 pad_maximum_fusion.1
  7.0 0.1 pad_maximum_fusion
  7.2 0.9 copy.58.sp_in
  8.1 0.0 copy-done.1
  8.1 0.8 copy.44
  8.9 0.0 copy-done.2
  8.9 0.8 copy.45
  9.7 0.0 copy-done.3
  9.7 0.1 reshape.265
  9.8 0.8 broadcast_in_dim.19.prop_in
  10.6 0.0 copy-done.4
  10.6 0.7 broadcast_in_dim.18.beta_in
  11.3 112.7 %shard_map.113 = (f32[4,96,256]{2,1,0:T(8,128)}, f32[8,128]{1,0:T(8,128)}) custom-call(f32[4,96,256]{2,1,0:T(8,128)} %bitcast.47, f32[4,96,256]{2,1,0:T(8,128)} %bitcast.48, f32[4,8,128]{2,1,0:T(8,128)} %broadcast_in_dim.18.beta_in, f32[4,96,128]{2,1,0:T(8,128)} %broadcast_in_dim.19.prop_in, bf16[8,48,256]{2,1,0:T(8,128)(2,1)} %copy.58.sp_in, ...), custom_call_target="tpu_custom_call" | custom-call | tf_op jit(solution)/shard_map/pallas_call | solution.py:510
  124.0 2.0 %copy.59 = f32[2,48,4,256]{3,2,1,0:T(4,128)} copy(f32[2,48,4,256]{3,1,0,2:T(8,128)} %bitcast.53) | data formatting | bytes 786432
  126.0 1.3 slice.39
  (16 shorter events, 0.3 us)
Async XLA Ops:
  0.6 6.3 %copy-start = (bf16[32,1,4,48,16]{3,4,2,1,0:T(8,128)(2,1)S(1)}, bf16[32,1,4,48,16]{3,4,2,1,0:T(8,128)(2,1)}, u32[]{:S(2)}) copy-start(bf16[32,1,4,48,16]{3,4,2,1,0:T(8,128)(2,1)} %param.14) | copy-start | bytes 589828
  5.4 2.7 %copy-start.1 = (f32[2,48,4,256]{3,2,1,0:T(4,128)S(1)}, f32[2,48,4,256]{3,2,1,0:T(4,128)}, u32[]{:S(2)}) copy-start(f32[2,48,4,256]{3,2,1,0:T(4,128)} %param.11) | copy-start | bytes 1179652
  5.7 3.3 %copy-start.2 = (f32[2,48,4,256]{3,2,1,0:T(4,128)S(1)}, f32[2,48,4,256]{3,2,1,0:T(4,128)}, u32[]{:S(2)}) copy-start(f32[2,48,4,256]{3,2,1,0:T(4,128)} %param.10) | copy-start | bytes 1179652
  6.9 2.8 %copy-start.3 = (f32[2,48,4]{1,2,0:T(4,128)S(1)}, f32[2,48,4]{1,2,0:T(4,128)}, u32[]{:S(2)}) copy-start(f32[2,48,4]{1,2,0:T(4,128)} %param.13) | copy-start | bytes 4612
  6.9 3.7 %copy-start.4 = (f32[4]{0:T(128)S(1)}, f32[4]{0:T(128)}, u32[]{:S(2)}) copy-start(f32[4]{0:T(128)} %param.12) | copy-start | bytes 52

commit v2 on v1

--- a/solution.py
+++ b/solution.py
@@ -21,6 +21,11 @@
 
 def place(x, yp, c):
     return (x * 4 + (yp + c) % 4) * 2 + c
+
+
+def owned(position):
+    _, yp, c = shifted(position)
+    return energy_of((yp % 2) * 2 + c, yp // 2)
 
 
 def energy_of(t, g):
@@ -59,13 +64,14 @@
     red_a,
     redt,
     red_b,
-    coefg,
+    red_c,
     sem_x,
     sem_in,
     sem_ag,
     sem_rs,
     sem_ra,
     sem_rb,
+    sem_rc,
     sem_fin,
 ):
     pa = lax.axis_index("pa")
@@ -89,10 +95,11 @@
 
     others = [(tme + d) % 4 for d in range(1, 4)]
     peers = [(j + d) % 8 for d in range(1, 8)]
+    plane = [(pa + d) % 32 for d in range(1, 32)]
     zs = [(z + d) % 8 for d in range(1, 8)]
 
     barrier = pltpu.get_barrier_semaphore()
-    friends = [member(t) for t in others] + [peer(p) for p in peers] + [(pa, q) for q in zs]
+    friends = [(q, z) for q in plane] + [(pa, q) for q in zs]
     for d in friends:
         pl.semaphore_signal(barrier, inc=1, device_id=d, device_id_type=MESH)
     pl.semaphore_wait(barrier, len(friends))
@@ -124,9 +131,10 @@
     q0g[tme] = q0_in[e]
     pg[tme] = prop_in[e]
 
+    h = 1 - g
     xr, xl, xo = (X + 1) % 4, (X + 3) % 4, (X + 2) % 4
-    dev_r, dev_l = peer(xr * 2 + g), peer(xl * 2 + g)
-    dev_p = peer(X * 2 + 1 - g)
+    dev_r, dev_l, dev_p = peer(xr * 2 + g), peer(xl * 2 + g), peer(X * 2 + h)
+    dev_rp, dev_lp = peer(xr * 2 + h), peer(xl * 2 + h)
 
     def ag_ref(it, t, slot, part):
         if part is None:
@@ -137,52 +145,46 @@
         slot, part, dev = (
             (j, None, dev_r),
             (j, None, dev_l),
+            (j, None, dev_p),
             (xl * 2 + g, 0, dev_r),
+            (xl * 2 + g, 0, dev_rp),
+            (xl * 2 + g, None, dev_p),
             (xr * 2 + g, 1, dev_l),
-            (j, None, dev_p),
-            (xl * 2 + g, None, dev_p),
+            (xr * 2 + g, 1, dev_lp),
             (xr * 2 + g, None, dev_p),
-            (xo * 2 + g, 0, dev_p),
-            (xo * 2 + g, 1, dev_p),
         )[k]
         ref = ag_ref(it, t, slot, part)
         return remote(ref, ref, sem_ag.at[it, 0, t, k], sem_ag.at[it, 1, t, k], dev)
 
     def ag_recv(it, t, k):
-        h = 1 - g
         slot, part = (
             (xl * 2 + g, None),
             (xr * 2 + g, None),
+            (X * 2 + h, None),
             (xo * 2 + g, 0),
+            (xo * 2 + h, 0),
+            (xl * 2 + h, None),
             (xo * 2 + g, 1),
-            (X * 2 + h, None),
-            (xl * 2 + h, None),
+            (xo * 2 + h, 1),
             (xr * 2 + h, None),
-            (xo * 2 + h, 0),
-            (xo * 2 + h, 1),
         )[k]
         ref = ag_ref(it, t, slot, part)
         remote(ref, ref, sem_ag.at[it, 0, t, k], sem_ag.at[it, 1, t, k], dev_p).wait_recv()
 
     def ag_first(it, t):
-        for k in (0, 1, 4):
+        for k in (0, 1, 2):
             ag_send(it, t, k).start()
 
     def ag_second(it, t):
         ag_recv(it, t, 0)
-        ag_send(it, t, 2).start()
-        ag_send(it, t, 5).start()
+        for k in (4, 3, 5):
+            ag_send(it, t, k).start()
         ag_recv(it, t, 1)
-        ag_send(it, t, 3).start()
-        ag_send(it, t, 6).start()
-
-    def ag_third(it, t):
-        for k in (2, 3):
-            ag_recv(it, t, k)
-            ag_send(it, t, k + 5).start()
+        for k in (7, 6, 8):
+            ag_send(it, t, k).start()
 
     def ag_last(it, t):
-        for k in (4, 5, 6, 7, 8):
+        for k in range(2, 9):
             ag_recv(it, t, k)
 
     row_ids = lax.broadcasted_iota(jnp.int32, (4 * ROWS, CH), 0)
@@ -238,6 +240,12 @@
         if step == 0:
             src = rs_s.at[it, way, 0, t, pl.ds(way * HALF, HALF)]
             dst = rs_r.at[it, way, 0, t, pl.ds(way * HALF, HALF)]
+        elif step == 1:
+            src = rs_s.at[it, way, 1, t, pl.ds(way * HALF, HALF)]
+            dst = rs_r.at[it, way, 1, t, pl.ds(way * HALF, HALF)]
+        elif step == 4:
+            src = rs_s.at[it, way, 1, t, pl.ds(HALF - way * HALF, HALF)]
+            dst = rs_r.at[it, way, 1, t, pl.ds(HALF - way * HALF, HALF)]
         else:
             src = rs_s.at[it, way, step, t]
             dst = rs_r.at[it, way, step, t]
@@ -254,23 +262,35 @@
             return carry
 
         lax.fori_loop(0, 4, one, 0)
+        couple(3)
+        couple(5)
+
+        def early(t, carry):
+            for way in range(2):
+                hi = HALF - way * HALF
+                rs_s[it, way, 1, t, hi : hi + HALF] = pbuf[3 + 2 * way, t, hi : hi + HALF].astype(bf16)
+                rs_copy(it, way, 4, t).start()
+            return carry
+
+        lax.fori_loop(0, 4, early, 0)
 
     def rs_step(it, step):
         rel = (4 - step, 4 + step)
-        couple(rel[0])
-        couple(rel[1])
+        if step > 1:
+            couple(rel[0])
+            couple(rel[1])
 
         def one(t, carry):
             for way in range(2):
                 rs_copy(it, way, step - 1, t).wait_recv()
                 if step == 1:
                     lo = way * HALF
-                    hi = HALF - lo
                     rs_s[it, way, 1, t, lo : lo + HALF] = (
                         pbuf[rel[way], t, lo : lo + HALF] + rs_r[it, way, 0, t, lo : lo + HALF].astype(f32)
                     ).astype(bf16)
-                    rs_s[it, way, 1, t, hi : hi + HALF] = pbuf[rel[way], t, hi : hi + HALF].astype(bf16)
                 else:
+                    if step == 2:
+                        rs_copy(it, way, 4, t).wait_recv()
                     rs_s[it, way, step, t] = (
                         pbuf[rel[way], t] + rs_r[it, way, step - 1, t].astype(f32)
                     ).astype(bf16)
@@ -305,6 +325,9 @@
         total = red_a[it, 0]
         for i in range(1, 8):
             total = total + red_a[it, i]
+        return total
+
+    def reduce_peers(it, total):
         redt[it] = total
         red_b[it, j] = total
         for p in peers:
@@ -313,9 +336,15 @@
     def reduce_last(it):
         for p in peers:
             rb_copy(it, p, p).wait_recv()
-        total = red_b[it, 0]
-        for i in range(1, 8):
-            total = total + red_b[it, i]
+        return finish([red_b[it, i] for i in range(8)])
+
+    def rc_copy(q, slot):
+        return remote(redt.at[1], red_c.at[slot], sem_rc.at[0, q], sem_rc.at[1, slot], (q, z))
+
+    def finish(tiles):
+        total = tiles[0]
+        for tile in tiles[1:]:
+            total = total + tile
         sums = jnp.sum(total, axis=1, keepdims=True)
         qw, ss, sq, qq = sums[0:1], sums[1:2], sums[2:3], sums[3:4]
         alpha = qw / CELLS
@@ -339,9 +368,6 @@
     for d in range(3):
         in_copy(0, d, others[d]).wait_recv()
         build(others[d])
-        if d == 0:
-            for t in order:
-                ag_third(0, t)
     for t in range(4):
         ag_last(0, t)
         spline_step(0, t, t == 0, t == 3)
@@ -373,18 +399,14 @@
     ag_second(1, 0)
     first_end(2)
     ag_second(1, 1)
-    ag_third(1, 0)
     first_end(3)
     reduce_first(0)
 
     ag_second(1, 2)
-    ag_third(1, 1)
     ag_second(1, 3)
-    ag_third(1, 2)
     ag_last(1, 0)
     spline_step(1, 0, True, False)
-    reduce_second(0)
-    ag_third(1, 3)
+    reduce_peers(0, reduce_second(0))
     for t in range(1, 4):
         ag_last(1, t)
         spline_step(1, t, False, t == 3)
@@ -394,8 +416,8 @@
 
     def fin_copy(kind, d, slot):
         t = others[d]
-        src = (q2g.at[t], s2g.at[t], coefg.at[e])[kind]
-        dst = (fin_q, fin_s, coefg)[kind].at[slot]
+        src = (q2g.at[t], s2g.at[t])[kind]
+        dst = (fin_q, fin_s)[kind].at[slot]
         return remote(src, dst, sem_fin.at[0, kind, d], sem_fin.at[1, kind, slot], member(t))
 
     for t in range(4):
@@ -420,31 +442,33 @@
     fin_s[e] = s2g[tme]
     for d in range(3):
         fin_copy(1, d, e).start()
-    reduce_second(1)
-    alpha2, rest2, beta2 = reduce_last(1)
+    total = reduce_second(1)
     wide = lambda v: jnp.broadcast_to(v, (1, 128))
-    coefg[e] = jnp.concatenate(
-        [wide(alpha1), wide(beta1), wide(alpha2), wide(beta2), jnp.zeros((4, 128), f32)], axis=0
-    )
-    for d in range(3):
-        fin_copy(2, d, e).start()
-    for kind in range(3):
+    total = jnp.concatenate([total[0:4], wide(alpha1), wide(beta1), total[6:8]], axis=0)
+    redt[1] = total
+    red_c[pa] = total
+    for q in plane:
+        rc_copy(q, pa).start()
+    for kind in range(2):
         for d in range(3):
             fin_copy(kind, d, energy_of(others[d], g)).wait_recv()
-    lanes = lax.broadcasted_iota(jnp.int32, (8, 128), 1)
-    table = jnp.zeros((8, 128), f32)
+    for q in plane:
+        rc_copy(q, q).wait_recv()
+    lanes = lax.broadcasted_iota(jnp.int32, (1, 128), 1)
+    lines = [jnp.zeros((1, 128), f32)] * 4
     for q in range(4):
-        mine = coefg[q]
-        table = jnp.where(lanes == q, mine, table)
-        rest = 1.0 - mine[2:3, 0:1]
-        out[q] = (fin_s[q] + rest * fin_q[q]) / mine[3:4, 0:1]
-    coef[...] = table
+        tiles = [red_c[i] for i in range(32) if owned(i) == q]
+        alpha2, rest2, beta2 = finish(tiles)
+        out[q] = (fin_s[q] + rest2 * fin_q[q]) / beta2
+        found = (tiles[0][4:5], tiles[0][5:6], wide(alpha2), wide(beta2))
+        lines = [jnp.where(lanes == q, new, old) for new, old in zip(found, lines)]
+    coef[...] = jnp.concatenate(lines, axis=0)[:, :4]
 
     for d in range(3):
         x_copy(d, tme).wait_send()
         for kind in range(4):
             in_copy(kind, d, tme).wait_send()
-        for kind in range(3):
+        for kind in range(2):
             fin_copy(kind, d, e).wait_send()
     for it in range(2):
 
@@ -452,15 +476,17 @@
             for k in range(9):
                 ag_send(it, t, k).wait_send()
             for way in range(2):
-                for step in range(4):
+                for step in range(5):
                     rs_copy(it, way, step, t).wait_send()
             return carry
 
         lax.fori_loop(0, 4, drain, 0)
         for q in zs:
             ra_copy(it, q, z).wait_send()
-        for p in peers:
-            rb_copy(it, p, j).wait_send()
+    for p in peers:
+        rb_copy(0, p, j).wait_send()
+    for q in plane:
+        rc_copy(q, pa).wait_send()
 
 
 def reorder(values):
@@ -511,7 +537,7 @@
         kernel,
         out_shape=(
             jax.ShapeDtypeStruct((4, ROWS, CH), f32),
-            jax.ShapeDtypeStruct((8, 128), f32),
+            jax.ShapeDtypeStruct((4, 4), f32),
         ),
         in_specs=[vmem] * 7,
         out_specs=(vmem, vmem),
@@ -538,21 +564,22 @@
             pltpu.VMEM((2, 8, 8, 128), f32),
             pltpu.VMEM((2, 8, 128), f32),
             pltpu.VMEM((2, 8, 8, 128), f32),
-            pltpu.VMEM((4, 8, 128), f32),
+            pltpu.VMEM((32, 8, 128), f32),
             dma((2, 4)),
             dma((2, 4, 4)),
             dma((2, 2, 4, 9)),
-            dma((2, 2, 2, 4, 4)),
+            dma((2, 2, 2, 5, 4)),
             dma((2, 2, 8)),
             dma((2, 2, 8)),
-            dma((2, 3, 4)),
+            dma((2, 32)),
+            dma((2, 2, 4)),
         ],
         compiler_params=pltpu.CompilerParams(
             collective_id=0, has_side_effects=True, vmem_limit_bytes=56 * 1024 * 1024
         ),
     )(q1, q0, beta, prop, tiles, meta, coupling)
     basis_next = out.transpose(1, 0, 2).reshape(2, 48, 4, CH)
-    return basis_next, coef[:4, :4]
+    return basis_next, coef
 
 
 def solution(mesh):

time: 128 us -> 121 us (0.945)
  Pallas kernels: 113 us -> 106 us
    pallas_call x1, Pallas kernels: 113 us -> 106 us  [body(): pl.pallas_call(kernel, out_shape=(jax.ShapeDtypeStruct((4, ROWS, CH), f32...]
    unnamed x18 -> x19, local copies, waits for them, and re-layouts: 7.23 us -> 8.49 us
where the time goes in v2:
time: 121 us
  Pallas kernels  106 us (88%)
  local copies, waits for them, and re-layouts  12.4 us (10%)
  other arithmetic  1.22 us (1%)
    pallas_call x1, Pallas kernels, body(): pl.pallas_call(kernel, out_shape=(jax.ShapeDtypeStruct((4, ROWS, CH), f32...  106 us
    unnamed x19, local copies, waits for them, and re-layouts  8.49 us

profile of v2, /device:TPU:1, one launch (start us, length us, event | category | flops | bytes accessed | tf_op | source)
XLA Modules:
  0.0 120.7 jit_solution(4698008239914995088)
XLA Ops:
  0.6 0.0 copy-start
  0.8 0.1 compare_and_fusion
  0.9 0.1 fusion
  0.9 0.9 copy.50
  1.9 0.9 copy.51
  2.8 0.9 copy.52
  3.7 0.8 copy.49
  4.6 0.6 gather_fusion
  5.2 0.1 copy.53
  5.3 0.1 broadcast_select_fusion
  5.4 0.1 fusion.2
  5.4 0.0 copy-start.1
  5.5 0.1 copy.56
  5.7 0.0 copy-start.2
  5.7 0.2 add.136
  5.9 0.2 add.137
  6.1 0.1 iota_add_fusion
  6.2 0.1 add.142
  6.3 0.6 broadcast_add_fusion.meta_in
  6.9 0.0 copy-done
  6.9 0.0 copy-start.3
  6.9 0.0 copy-start.4
  7.0 0.1 pad_maximum_fusion.1
  7.0 0.1 pad_maximum_fusion
  7.2 0.9 copy.58.sp_in
  8.1 0.0 copy-done.1
  8.1 0.8 copy.44
  8.9 0.0 copy-done.2
  8.9 0.8 copy.45
  9.7 0.0 copy-done.3
  9.7 0.1 reshape.265
  9.8 0.8 broadcast_in_dim.19.prop_in
  10.6 0.0 copy-done.4
  10.6 0.7 broadcast_in_dim.18.beta_in
  11.3 106.1 %shard_map.113 = (f32[4,96,256]{2,1,0:T(8,128)}, f32[4,4]{1,0:T(4,128)}) custom-call(f32[4,96,256]{2,1,0:T(8,128)} %bitcast.47, f32[4,96,256]{2,1,0:T(8,128)} %bitcast.48, f32[4,8,128]{2,1,0:T(8,128)} %broadcast_in_dim.18.beta_in, f32[4,96,128]{2,1,0:T(8,128)} %broadcast_in_dim.19.prop_in, bf16[8,48,256]{2,1,0:T(8,128)(2,1)} %copy.58.sp_in, ...), custom_call_target="tpu_custom_call" | custom-call | tf_op jit(solution)/shard_map/pallas_call | solution.py:536
  117.4 2.0 %copy.59 = f32[2,48,4,256]{3,2,1,0:T(4,128)} copy(f32[2,48,4,256]{3,1,0,2:T(8,128)} %bitcast.53) | data formatting | bytes 786432
  119.4 1.3 %copy.64 = f32[4,4]{1,0:T(4,128)} copy(f32[4,4]{1,0:T(4,128)} %get-tuple-element.21) | data formatting | bytes 128
  (16 shorter events, 0.3 us)
Async XLA Ops:
  0.6 6.3 %copy-start = (bf16[32,1,4,48,16]{3,4,2,1,0:T(8,128)(2,1)S(1)}, bf16[32,1,4,48,16]{3,4,2,1,0:T(8,128)(2,1)}, u32[]{:S(2)}) copy-start(bf16[32,1,4,48,16]{3,4,2,1,0:T(8,128)(2,1)} %param.14) | copy-start | bytes 589828
  5.4 2.7 %copy-start.1 = (f32[2,48,4,256]{3,2,1,0:T(4,128)S(1)}, f32[2,48,4,256]{3,2,1,0:T(4,128)}, u32[]{:S(2)}) copy-start(f32[2,48,4,256]{3,2,1,0:T(4,128)} %param.11) | copy-start | bytes 1179652
  5.7 3.3 %copy-start.2 = (f32[2,48,4,256]{3,2,1,0:T(4,128)S(1)}, f32[2,48,4,256]{3,2,1,0:T(4,128)}, u32[]{:S(2)}) copy-start(f32[2,48,4,256]{3,2,1,0:T(4,128)} %param.10) | copy-start | bytes 1179652
  6.9 2.8 %copy-start.3 = (f32[2,48,4]{1,2,0:T(4,128)S(1)}, f32[2,48,4]{1,2,0:T(4,128)}, u32[]{:S(2)}) copy-start(f32[2,48,4]{1,2,0:T(4,128)} %param.13) | copy-start | bytes 4612
  6.9 3.7 %copy-start.4 = (f32[4]{0:T(128)S(1)}, f32[4]{0:T(128)}, u32[]{:S(2)}) copy-start(f32[4]{0:T(128)} %param.12) | copy-start | bytes 52

commit v3 on v2

--- a/solution.py
+++ b/solution.py
@@ -32,16 +32,73 @@
     return (t % 2) * 2 + 1 - (t // 2 + g) % 2
 
 
+def source(b, spot):
+    th, c = b // 4, (b // 2) % 2
+    x = (b % 2) * 2 + (spot >> 1)
+    return x * 8 + ((2 * (spot & 1) + th + c) & 3) * 2 + c
+
+
+def split_energies(raw, parts):
+    for q in range(4):
+        parts[q] = raw[:, :, q, :].reshape(ROWS, CH)
+
+
+def turn_tiles(raw, tiles):
+    for b in range(8):
+        rows = [raw[source(b, i) * 64 : source(b, i) * 64 + 64, :] for i in range(4)]
+        block = jnp.concatenate(rows, axis=0).astype(jnp.float32)
+        tiles[b] = jnp.transpose(block).astype(jnp.bfloat16)
+
+
+def spread_edges(edges, meta, x, g):
+    n = lax.broadcasted_iota(jnp.int32, (8, 32), 0)
+    r = lax.broadcasted_iota(jnp.int32, (8, 32), 1)
+    target = (x * 4 + ((2 * g + ((n >> 1) & 1) + (n & 1)) & 3)) * 2 + (n & 1)
+    pick = jnp.where(r == target, 1.0, 0.0).astype(jnp.bfloat16)
+    over = (((1,), (1,)), ((), ()))
+    found = [
+        lax.dot_general(pick, edges[i].astype(jnp.bfloat16), over, preferred_element_type=jnp.float32)
+        for i in range(2)
+    ]
+    found = jnp.concatenate(found, axis=0).astype(jnp.bfloat16)
+    col = lax.broadcasted_iota(jnp.int32, (128, CH), 1)
+    row = lax.broadcasted_iota(jnp.int32, (128, CH), 0)
+    lane = lax.broadcasted_iota(jnp.int32, (8, CH), 1)
+    for b in range(8):
+        wanted = source(b, col >> 6) * 4 + ((col >> 4) & 3)
+        widen = jnp.where(row == wanted, 1.0, 0.0).astype(jnp.bfloat16)
+        both = jnp.dot(found, widen, preferred_element_type=jnp.float32).astype(jnp.int32)
+        meta[b] = both[0:8] * 1024 + both[8:16] + (lane >> 6) * ROWS + (lane & 15)
+
+
+def spread_propagator(raw, square, parts):
+    square[...] = jnp.zeros_like(square)
+    for p in range(2):
+        square[p * 8 : p * 8 + 4, 0:HALF] = raw[p]
+    turned = jnp.transpose(square[...])
+    for p in range(2):
+        for q in range(4):
+            line = turned[0:HALF, p * 8 + q : p * 8 + q + 1]
+            parts[q, p * HALF : (p + 1) * HALF, :] = jnp.broadcast_to(line, (HALF, 128))
+
+
 def kernel(
+    q1_raw,
+    q0_raw,
+    beta_in,
+    prop_raw,
+    sp_raw,
+    edges,
+    cpl_hbm,
+    out,
+    coef,
+    cpl,
     q1_in,
     q0_in,
-    beta_in,
     prop_in,
+    square,
     sp_in,
     meta_in,
-    cpl,
-    out,
-    coef,
     xs,
     spg,
     dmat,
@@ -73,6 +130,7 @@
     sem_rb,
     sem_rc,
     sem_fin,
+    sem_cpl,
 ):
     pa = lax.axis_index("pa")
     z = lax.axis_index("ch")
@@ -102,6 +160,9 @@
     friends = [(q, z) for q in plane] + [(pa, q) for q in zs]
     for d in friends:
         pl.semaphore_signal(barrier, inc=1, device_id=d, device_id_type=MESH)
+    coupling_copy = pltpu.make_async_copy(cpl_hbm, cpl, sem_cpl)
+    coupling_copy.start()
+    split_energies(q1_raw, q1_in)
     pl.semaphore_wait(barrier, len(friends))
 
     def remote(src, dst, send, recv, device):
@@ -123,13 +184,11 @@
     for d in range(3):
         xs[d] = q1_in[energy_of(others[d], g)].astype(bf16)
         x_copy(d, tme).start()
+    xg[0, tme, j] = q1_in[e].astype(bf16)
+    turn_tiles(sp_raw, sp_in)
     for d in range(3):
         in_copy(0, d, tme).start()
-    xg[0, tme, j] = q1_in[e].astype(bf16)
     spg[tme] = sp_in[...]
-    q1g[tme] = q1_in[e]
-    q0g[tme] = q0_in[e]
-    pg[tme] = prop_in[e]
 
     h = 1 - g
     xr, xl, xo = (X + 1) % 4, (X + 3) % 4, (X + 2) % 4
@@ -193,7 +252,7 @@
         def one(ts, carry):
             for half in range(2):
                 b = ts * 2 + half
-                meta = meta_in[tt, b]
+                meta = meta_in[b, pl.ds(tt, 1), :]
                 key = lax.shift_right_logical(meta, 10)
                 row = meta & 1023
                 tile = spg[tt, b]
@@ -358,10 +417,16 @@
     for d in range(3):
         x_copy(d, others[d]).wait_recv()
         ag_first(0, others[d])
+    spread_edges(edges, meta_in, X, g)
     build(tme)
     order = [tme] + others
     for t in order:
         ag_second(0, t)
+    split_energies(q0_raw, q0_in)
+    spread_propagator(prop_raw, square, prop_in)
+    q1g[tme] = q1_in[e]
+    q0g[tme] = q0_in[e]
+    pg[tme] = prop_in[e]
     for kind in (1, 2, 3):
         for d in range(3):
             in_copy(kind, d, tme).start()
@@ -371,6 +436,7 @@
     for t in range(4):
         ag_last(0, t)
         spline_step(0, t, t == 0, t == 3)
+    coupling_copy.wait()
     rs_begin(0)
     for step in (1, 2, 3):
         rs_step(0, step)
@@ -378,7 +444,7 @@
     for kind in (1, 2, 3):
         for d in range(3):
             in_copy(kind, d, others[d]).wait_recv()
-    beta0 = beta_in[e][0:1, 0:1]
+    beta0 = beta_in[e]
 
     def first_end(t):
         y = rs_end(0, t)
@@ -459,7 +525,7 @@
     for q in range(4):
         tiles = [red_c[i] for i in range(32) if owned(i) == q]
         alpha2, rest2, beta2 = finish(tiles)
-        out[q] = (fin_s[q] + rest2 * fin_q[q]) / beta2
+        out[:, :, q, :] = ((fin_s[q] + rest2 * fin_q[q]) / beta2).reshape(2, HALF, CH)
         found = (tiles[0][4:5], tiles[0][5:6], wide(alpha2), wide(beta2))
         lines = [jnp.where(lanes == q, new, old) for new, old in zip(found, lines)]
     coef[...] = jnp.concatenate(lines, axis=0)[:, :4]
@@ -487,15 +553,6 @@
         rb_copy(0, p, j).wait_send()
     for q in plane:
         rc_copy(q, pa).wait_send()
-
-
-def reorder(values):
-    tail = values.shape[1:]
-    values = values.reshape((4, 4, 2) + tail)
-    values = jnp.stack([values[:, :, 0], jnp.roll(values[:, :, 1], -1, axis=1)], axis=2)
-    values = values.reshape((2, 2, 2, 2, 2) + tail)
-    rest = tuple(range(5, 5 + len(tail)))
-    return values.transpose((3, 4, 0, 1, 2) + rest).reshape((8, 4) + tail)
 
 
 def body(
@@ -512,36 +569,38 @@
 ):
     f32 = jnp.float32
     bf16 = jnp.bfloat16
-    by_energy = lambda v: v.reshape(ROWS, 4, CH).transpose(1, 0, 2)
-    q1 = by_energy(basis_now)
-    q0 = by_energy(basis_prev)
-    prop = jnp.broadcast_to(propagator.reshape(ROWS, 4).T[:, :, None], (4, ROWS, 128))
-    beta = jnp.broadcast_to(beta_prev[:, None, None], (4, 8, 128))
-    tiles = reorder(spline[:, 0])
-    tiles = tiles.transpose(0, 3, 1, 2, 4).reshape(8, HALF, CH)
-
-    X, yp, _ = shifted(lax.axis_index("pa"))
-    targets = jnp.stack([place(X, 2 * (yp // 2) + t // 2, t % 2) for t in range(4)])
-    live = jnp.arange(4, dtype=jnp.int32)[None, None, :] < edge_count[:, :, None]
-    packed = jnp.where(live, edge_term * 2 + edge_tile, 6) * 1024 + edge_offset
-    packed = reorder(jnp.take(packed, targets, axis=1))
-    packed = packed.transpose(2, 0, 1, 3)[..., None]
-    shift = (
-        jnp.arange(4, dtype=jnp.int32)[:, None, None] * ROWS + jnp.arange(16, dtype=jnp.int32)[None, None, :]
-    )
-    meta = (packed + shift).reshape(4, 8, 1, CH)
+    tiles = spline.transpose(0, 1, 2, 4, 3).reshape(2048, HALF)
+    live = jnp.arange(4, dtype=jnp.int32)[None, :, None] < edge_count[:, None, :]
+    flat = lambda v: v.transpose(0, 2, 1)
+    key = jnp.where(live, flat(edge_term) * 2 + flat(edge_tile), 6)
+    edges = jnp.stack([key.reshape(128, 32), flat(edge_offset).reshape(128, 32)]).astype(f32)
 
     vmem = pl.BlockSpec(memory_space=pltpu.VMEM)
     dma = pltpu.SemaphoreType.DMA
     out, coef = pl.pallas_call(
         kernel,
         out_shape=(
-            jax.ShapeDtypeStruct((4, ROWS, CH), f32),
+            jax.ShapeDtypeStruct((2, HALF, 4, CH), f32),
             jax.ShapeDtypeStruct((4, 4), f32),
         ),
-        in_specs=[vmem] * 7,
+        in_specs=[
+            vmem,
+            vmem,
+            pl.BlockSpec(memory_space=pltpu.SMEM),
+            vmem,
+            vmem,
+            vmem,
+            pl.BlockSpec(memory_space=pl.ANY),
+        ],
         out_specs=(vmem, vmem),
         scratch_shapes=[
+            pltpu.VMEM((3, 2048, CH), bf16),
+            pltpu.VMEM((4, ROWS, CH), f32),
+            pltpu.VMEM((4, ROWS, CH), f32),
+            pltpu.VMEM((4, ROWS, 128), f32),
+            pltpu.VMEM((128, 128), f32),
+            pltpu.VMEM((8, HALF, CH), bf16),
+            pltpu.VMEM((8, 8, CH), jnp.int32),
             pltpu.VMEM((3, ROWS, CH), bf16),
             pltpu.VMEM((4, 8, HALF, CH), bf16),
             pltpu.VMEM((4, 4, 288, 768), bf16),
@@ -573,13 +632,13 @@
             dma((2, 2, 8)),
             dma((2, 32)),
             dma((2, 2, 4)),
+            dma(()),
         ],
         compiler_params=pltpu.CompilerParams(
             collective_id=0, has_side_effects=True, vmem_limit_bytes=56 * 1024 * 1024
         ),
-    )(q1, q0, beta, prop, tiles, meta, coupling)
-    basis_next = out.transpose(1, 0, 2).reshape(2, 48, 4, CH)
-    return basis_next, coef
+    )(basis_now, basis_prev, beta_prev, propagator.transpose(0, 2, 1), tiles, edges, coupling)
+    return out, coef
 
 
 def solution(mesh):

time: 121 us -> 112 us (0.926)
  local copies, waits for them, and re-layouts: 12.4 us -> 3 us
    unnamed x19 -> x2, local copies, waits for them, and re-layouts: 8.49 us -> 3 us
    convert_element_type x0 -> x1, other arithmetic: none -> 1.51 us  [body(): jnp.stack([key.reshape(128, 32), flat(edge_offset).reshape(128, 32)])]
    broadcast_in_dim x2 -> x0, local copies, waits for them, and re-layouts: 1.46 us -> none  [the longest x1 0.79 us: body(): jnp.broadcast_to(propagator.reshape(ROWS, 4).T[:, :, None], (4, ROWS, 128))]
where the time goes in v3:
time: 112 us
  Pallas kernels  106 us (95%)
  local copies, waits for them, and re-layouts  3 us (3%)
  other arithmetic  2.41 us (2%)
    pallas_call x1, Pallas kernels, body(): pl.pallas_call(kernel, out_shape=(jax.ShapeDtypeStruct((2, HALF, 4, CH),...  106 us
    unnamed x2, local copies, waits for them, and re-layouts  3 us

profile of v3, /device:TPU:1, one launch (start us, length us, event | category | flops | bytes accessed | tf_op | source)
XLA Modules:
  0.0 111.6 jit_solution(13100262867493065577)
XLA Ops:
  0.6 0.9 bitcast_select_fusion
  1.5 1.5 %add_convert_fusion.edges = f32[2,128,32]{2,1,0:T(8,128)} fusion(s32[1,128,32]{2,1,0:T(8,128)} %bitcast.12, s32[1,128,32]{2,1,0:T(8,128)S(1)} %bitcast.11), kind=kLoop, calls=%fused_computation | loop fusion | flops 16384 | bytes 65536 | tf_op jit(solution)/shard_map/convert_element_type | solution.py:576
  3.0 105.6 %shard_map.113 = (f32[2,48,4,256]{3,2,1,0:T(4,128)}, f32[4,4]{1,0:T(4,128)}) custom-call(f32[2,48,4,256]{3,2,1,0:T(4,128)} %q1_raw.1, f32[2,48,4,256]{3,2,1,0:T(4,128)} %q0_raw.1, f32[4]{0:T(128)} %beta_in.1, f32[2,4,48]{2,1,0:T(4,128)} %bitcast.13, bf16[2048,48]{1,0:T(8,128)(2,1)} %bitcast.10, f32[2,128,32]{2,1,0:T(8,128)} %add_convert_fusion.edges, ...), custom_call_target="tpu_custom_call" | custom-call | tf_op jit(solution)/shard_map/pallas_call | solution.py:580
  108.6 1.8 %copy.20 = f32[2,48,4,256]{3,2,1,0:T(4,128)} copy(f32[2,48,4,256]{3,2,1,0:T(4,128)} %get-tuple-element.4) | data formatting | bytes 786432
  110.4 1.2 %copy.21 = f32[4,4]{1,0:T(4,128)} copy(f32[4,4]{1,0:T(4,128)} %get-tuple-element.5) | data formatting | bytes 128

commit v4 on v3

--- a/solution.py
+++ b/solution.py
@@ -50,22 +50,24 @@
         tiles[b] = jnp.transpose(block).astype(jnp.bfloat16)
 
 
-def spread_edges(edges, meta, x, g):
+def spread_edges(offsets, tiles, terms, counts, meta, x, g):
     n = lax.broadcasted_iota(jnp.int32, (8, 32), 0)
     r = lax.broadcasted_iota(jnp.int32, (8, 32), 1)
     target = (x * 4 + ((2 * g + ((n >> 1) & 1) + (n & 1)) & 3)) * 2 + (n & 1)
     pick = jnp.where(r == target, 1.0, 0.0).astype(jnp.bfloat16)
     over = (((1,), (1,)), ((), ()))
-    found = [
-        lax.dot_general(pick, edges[i].astype(jnp.bfloat16), over, preferred_element_type=jnp.float32)
-        for i in range(2)
-    ]
-    found = jnp.concatenate(found, axis=0).astype(jnp.bfloat16)
+    found = []
+    for slot in range(4):
+        key = jnp.where(slot < counts[...], terms[:, slot, :] * 2 + tiles[:, slot, :], 6)
+        both = jnp.concatenate([key, offsets[:, slot, :]], axis=0).astype(jnp.float32).astype(jnp.bfloat16)
+        both = lax.dot_general(pick, both, over, preferred_element_type=jnp.float32)
+        found.append(jnp.concatenate([both[:, 0:32], both[:, 32:64]], axis=0))
+    found = jnp.concatenate(found, axis=1).astype(jnp.bfloat16)
     col = lax.broadcasted_iota(jnp.int32, (128, CH), 1)
     row = lax.broadcasted_iota(jnp.int32, (128, CH), 0)
     lane = lax.broadcasted_iota(jnp.int32, (8, CH), 1)
     for b in range(8):
-        wanted = source(b, col >> 6) * 4 + ((col >> 4) & 3)
+        wanted = source(b, col >> 6) + ((col >> 4) & 3) * 32
         widen = jnp.where(row == wanted, 1.0, 0.0).astype(jnp.bfloat16)
         both = jnp.dot(found, widen, preferred_element_type=jnp.float32).astype(jnp.int32)
         meta[b] = both[0:8] * 1024 + both[8:16] + (lane >> 6) * ROWS + (lane & 15)
@@ -88,7 +90,10 @@
     beta_in,
     prop_raw,
     sp_raw,
-    edges,
+    offset_raw,
+    tile_raw,
+    term_raw,
+    count_raw,
     cpl_hbm,
     out,
     coef,
@@ -207,10 +212,10 @@
             (j, None, dev_p),
             (xl * 2 + g, 0, dev_r),
             (xl * 2 + g, 0, dev_rp),
-            (xl * 2 + g, None, dev_p),
+            ((xl * 2 + g, None, dev_p), (X * 2 + h, None, dev_r))[it == 0],
             (xr * 2 + g, 1, dev_l),
             (xr * 2 + g, 1, dev_lp),
-            (xr * 2 + g, None, dev_p),
+            ((xr * 2 + g, None, dev_p), (X * 2 + h, None, dev_l))[it == 0],
         )[k]
         ref = ag_ref(it, t, slot, part)
         return remote(ref, ref, sem_ag.at[it, 0, t, k], sem_ag.at[it, 1, t, k], dev)
@@ -235,15 +240,17 @@
             ag_send(it, t, k).start()
 
     def ag_second(it, t):
-        ag_recv(it, t, 0)
-        for k in (4, 3, 5):
-            ag_send(it, t, k).start()
-        ag_recv(it, t, 1)
-        for k in (7, 6, 8):
-            ag_send(it, t, k).start()
+        if it == 0:
+            steps = ((0, (4, 3)), (1, (7, 6)), (2, (5, 8)))
+        else:
+            steps = ((0, (4, 3, 5)), (1, (7, 6, 8)))
+        for arrived, onward in steps:
+            ag_recv(it, t, arrived)
+            for k in onward:
+                ag_send(it, t, k).start()
 
     def ag_last(it, t):
-        for k in range(2, 9):
+        for k in range(3 if it == 0 else 2, 9):
             ag_recv(it, t, k)
 
     row_ids = lax.broadcasted_iota(jnp.int32, (4 * ROWS, CH), 0)
@@ -417,7 +424,7 @@
     for d in range(3):
         x_copy(d, others[d]).wait_recv()
         ag_first(0, others[d])
-    spread_edges(edges, meta_in, X, g)
+    spread_edges(offset_raw, tile_raw, term_raw, count_raw, meta_in, X, g)
     build(tme)
     order = [tme] + others
     for t in order:
@@ -427,9 +434,6 @@
     q1g[tme] = q1_in[e]
     q0g[tme] = q0_in[e]
     pg[tme] = prop_in[e]
-    for kind in (1, 2, 3):
-        for d in range(3):
-            in_copy(kind, d, tme).start()
     for d in range(3):
         in_copy(0, d, others[d]).wait_recv()
         build(others[d])
@@ -438,6 +442,9 @@
         spline_step(0, t, t == 0, t == 3)
     coupling_copy.wait()
     rs_begin(0)
+    for kind in (1, 2, 3):
+        for d in range(3):
+            in_copy(kind, d, tme).start()
     for step in (1, 2, 3):
         rs_step(0, step)
     couple(0)
@@ -570,10 +577,7 @@
     f32 = jnp.float32
     bf16 = jnp.bfloat16
     tiles = spline.transpose(0, 1, 2, 4, 3).reshape(2048, HALF)
-    live = jnp.arange(4, dtype=jnp.int32)[None, :, None] < edge_count[:, None, :]
     flat = lambda v: v.transpose(0, 2, 1)
-    key = jnp.where(live, flat(edge_term) * 2 + flat(edge_tile), 6)
-    edges = jnp.stack([key.reshape(128, 32), flat(edge_offset).reshape(128, 32)]).astype(f32)
 
     vmem = pl.BlockSpec(memory_space=pltpu.VMEM)
     dma = pltpu.SemaphoreType.DMA
@@ -587,6 +591,9 @@
             vmem,
             vmem,
             pl.BlockSpec(memory_space=pltpu.SMEM),
+            vmem,
+            vmem,
+            vmem,
             vmem,
             vmem,
             vmem,
@@ -637,7 +644,18 @@
         compiler_params=pltpu.CompilerParams(
             collective_id=0, has_side_effects=True, vmem_limit_bytes=56 * 1024 * 1024
         ),
-    )(basis_now, basis_prev, beta_prev, propagator.transpose(0, 2, 1), tiles, edges, coupling)
+    )(
+        basis_now,
+        basis_prev,
+        beta_prev,
+        flat(propagator),
+        tiles,
+        flat(edge_offset),
+        flat(edge_tile),
+        flat(edge_term),
+        edge_count,
+        coupling,
+    )
     return out, coef
 
 

time: 112 us -> 105 us (0.938)
  Pallas kernels: 106 us -> 101 us
  other arithmetic: 2.41 us -> 0 us
    pallas_call x1, Pallas kernels: 106 us -> 101 us  [body(): pl.pallas_call(kernel, out_shape=(jax.ShapeDtypeStruct((2, HALF, 4, CH),...]
    convert_element_type x1 -> x0, other arithmetic: 1.51 us -> none  [body(): jnp.stack([key.reshape(128, 32), flat(edge_offset).reshape(128, 32)])]
where the time goes in v4:
time: 105 us
  Pallas kernels  101 us (96%)
  local copies, waits for them, and re-layouts  3 us (3%)
    pallas_call x1, Pallas kernels, body(): pl.pallas_call(kernel, out_shape=(jax.ShapeDtypeStruct((2, HALF, 4, CH),...  101 us
    unnamed x2, local copies, waits for them, and re-layouts  3 us

profile of v4, /device:TPU:1, one launch (start us, length us, event | category | flops | bytes accessed | tf_op | source)
XLA Modules:
  0.0 104.8 jit_solution(16638724243068809362)
XLA Ops:
  0.6 101.1 %shard_map.113 = (f32[2,48,4,256]{3,2,1,0:T(4,128)}, f32[4,4]{1,0:T(4,128)}) custom-call(f32[2,48,4,256]{3,2,1,0:T(4,128)} %q1_raw.1, f32[2,48,4,256]{3,2,1,0:T(4,128)} %q0_raw.1, f32[4]{0:T(128)} %beta_in.1, f32[2,4,48]{2,1,0:T(4,128)} %bitcast.11, bf16[2048,48]{1,0:T(8,128)(2,1)} %bitcast.7, s32[32,4,32]{2,1,0:T(4,128)} %bitcast.8, s32[32,4,32]{2,1,0:T(4,128)} %bitcast.9, ...), custom_call_target="tpu_custom_call" | custom-call | tf_op jit(solution)/shard_map/pallas_call | solution.py:584
  101.8 1.8 %copy.14 = f32[2,48,4,256]{3,2,1,0:T(4,128)} copy(f32[2,48,4,256]{3,2,1,0:T(4,128)} %get-tuple-element.4) | data formatting | bytes 786432
  103.5 1.2 %copy.15 = f32[4,4]{1,0:T(4,128)} copy(f32[4,4]{1,0:T(4,128)} %get-tuple-element.5) | data formatting | bytes 128

commit v5 on v4

--- a/solution.py
+++ b/solution.py
@@ -85,19 +85,25 @@
 
 
 def kernel(
-    q1_raw,
-    q0_raw,
+    q1_raw_hbm,
+    q0_raw_hbm,
     beta_in,
     prop_raw,
-    sp_raw,
-    offset_raw,
-    tile_raw,
-    term_raw,
+    sp_raw_hbm,
+    offset_raw_hbm,
+    tile_raw_hbm,
+    term_raw_hbm,
     count_raw,
     cpl_hbm,
     out,
     coef,
     cpl,
+    q1_raw,
+    q0_raw,
+    sp_raw,
+    offset_raw,
+    tile_raw,
+    term_raw,
     q1_in,
     q0_in,
     prop_in,
@@ -136,6 +142,7 @@
     sem_rc,
     sem_fin,
     sem_cpl,
+    sem_load,
 ):
     pa = lax.axis_index("pa")
     z = lax.axis_index("ch")
@@ -166,7 +173,19 @@
     for d in friends:
         pl.semaphore_signal(barrier, inc=1, device_id=d, device_id_type=MESH)
     coupling_copy = pltpu.make_async_copy(cpl_hbm, cpl, sem_cpl)
+    pairs = (
+        (q1_raw_hbm, q1_raw),
+        (sp_raw_hbm, sp_raw),
+        (offset_raw_hbm, offset_raw),
+        (tile_raw_hbm, tile_raw),
+        (term_raw_hbm, term_raw),
+        (q0_raw_hbm, q0_raw),
+    )
+    loads = [pltpu.make_async_copy(src, dst, sem_load.at[i]) for i, (src, dst) in enumerate(pairs)]
+    for load in loads:
+        load.start()
     coupling_copy.start()
+    loads[0].wait()
     split_energies(q1_raw, q1_in)
     pl.semaphore_wait(barrier, len(friends))
 
@@ -190,6 +209,7 @@
         xs[d] = q1_in[energy_of(others[d], g)].astype(bf16)
         x_copy(d, tme).start()
     xg[0, tme, j] = q1_in[e].astype(bf16)
+    loads[1].wait()
     turn_tiles(sp_raw, sp_in)
     for d in range(3):
         in_copy(0, d, tme).start()
@@ -339,12 +359,11 @@
             return carry
 
         lax.fori_loop(0, 4, early, 0)
+        for r in (2, 6, 1, 7, 0):
+            couple(r)
 
     def rs_step(it, step):
         rel = (4 - step, 4 + step)
-        if step > 1:
-            couple(rel[0])
-            couple(rel[1])
 
         def one(t, carry):
             for way in range(2):
@@ -424,11 +443,14 @@
     for d in range(3):
         x_copy(d, others[d]).wait_recv()
         ag_first(0, others[d])
+    for load in loads[2:5]:
+        load.wait()
     spread_edges(offset_raw, tile_raw, term_raw, count_raw, meta_in, X, g)
     build(tme)
     order = [tme] + others
     for t in order:
         ag_second(0, t)
+    loads[5].wait()
     split_energies(q0_raw, q0_in)
     spread_propagator(prop_raw, square, prop_in)
     q1g[tme] = q1_in[e]
@@ -447,7 +469,6 @@
             in_copy(kind, d, tme).start()
     for step in (1, 2, 3):
         rs_step(0, step)
-    couple(0)
     for kind in (1, 2, 3):
         for d in range(3):
             in_copy(kind, d, others[d]).wait_recv()
@@ -500,7 +521,6 @@
         fin_copy(0, d, e).start()
     rs_step(1, 2)
     rs_step(1, 3)
-    couple(0)
     for t in range(4):
         y = (rs_end(1, t) + rest1 * y1g[t]) / beta1
         q2 = q2g[t]
@@ -562,6 +582,11 @@
         rc_copy(q, pa).wait_send()
 
 
+def hand_over(out_in, coef_in, out, coef):
+    out[...] = out_in[...]
+    coef[...] = coef_in[...]
+
+
 def body(
     basis_prev,
     basis_now,
@@ -580,6 +605,7 @@
     flat = lambda v: v.transpose(0, 2, 1)
 
     vmem = pl.BlockSpec(memory_space=pltpu.VMEM)
+    anywhere = pl.BlockSpec(memory_space=pl.ANY)
     dma = pltpu.SemaphoreType.DMA
     out, coef = pl.pallas_call(
         kernel,
@@ -588,20 +614,26 @@
             jax.ShapeDtypeStruct((4, 4), f32),
         ),
         in_specs=[
-            vmem,
-            vmem,
+            anywhere,
+            anywhere,
             pl.BlockSpec(memory_space=pltpu.SMEM),
             vmem,
+            anywhere,
+            anywhere,
+            anywhere,
+            anywhere,
             vmem,
-            vmem,
-            vmem,
-            vmem,
-            vmem,
-            pl.BlockSpec(memory_space=pl.ANY),
+            anywhere,
         ],
         out_specs=(vmem, vmem),
         scratch_shapes=[
             pltpu.VMEM((3, 2048, CH), bf16),
+            pltpu.VMEM((2, HALF, 4, CH), f32),
+            pltpu.VMEM((2, HALF, 4, CH), f32),
+            pltpu.VMEM((2048, HALF), bf16),
+            pltpu.VMEM((32, 4, 32), jnp.int32),
+            pltpu.VMEM((32, 4, 32), jnp.int32),
+            pltpu.VMEM((32, 4, 32), jnp.int32),
             pltpu.VMEM((4, ROWS, CH), f32),
             pltpu.VMEM((4, ROWS, CH), f32),
             pltpu.VMEM((4, ROWS, 128), f32),
@@ -640,6 +672,7 @@
             dma((2, 32)),
             dma((2, 2, 4)),
             dma(()),
+            dma((6,)),
         ],
         compiler_params=pltpu.CompilerParams(
             collective_id=0, has_side_effects=True, vmem_limit_bytes=56 * 1024 * 1024
@@ -656,7 +689,13 @@
         edge_count,
         coupling,
     )
-    return out, coef
+    shapes = (jax.ShapeDtypeStruct((2, HALF, 4, CH), f32), jax.ShapeDtypeStruct((4, 4), f32))
+    return pl.pallas_call(
+        hand_over,
+        out_shape=shapes,
+        in_specs=[vmem] * 2,
+        out_specs=(vmem, vmem),
+    )(out, coef)
 
 
 def solution(mesh):

time: 105 us -> 103 us (0.981)
  local copies, waits for them, and re-layouts: 3 us -> 0 us
    unnamed x2 -> x0, local copies, waits for them, and re-layouts: 3 us -> none
    pallas_call x0 -> x1, Pallas kernels: none -> 1.77 us  [body(): pl.pallas_call(hand_over, out_shape=shapes, in_specs=[vmem] * 2, out_spec...]
where the time goes in v5:
time: 103 us
  Pallas kernels  102 us (99%)
    pallas_call x1, Pallas kernels, body(): pl.pallas_call(kernel, out_shape=(jax.ShapeDtypeStruct((2, HALF, 4, CH),...  100 us

profile of v5, /device:TPU:1, one launch (start us, length us, event | category | flops | bytes accessed | tf_op | source)
XLA Modules:
  0.0 102.7 jit_solution(9296391845238254655)
XLA Ops:
  0.6 100.2 %shard_map.113 = (f32[2,48,4,256]{3,2,1,0:T(4,128)}, f32[4,4]{1,0:T(4,128)}) custom-call(f32[2,48,4,256]{3,2,1,0:T(4,128)} %q1_raw_hbm.1, f32[2,48,4,256]{3,2,1,0:T(4,128)} %q0_raw_hbm.1, f32[4]{0:T(128)} %beta_in.1, f32[2,4,48]{2,1,0:T(4,128)} %bitcast.11, bf16[2048,48]{1,0:T(8,128)(2,1)} %bitcast.7, s32[32,4,32]{2,1,0:T(4,128)} %bitcast.8, ...), custom_call_target="tpu_custom_call" | custom-call | tf_op jit(solution)/shard_map/pallas_call | solution.py:610
  100.9 1.8 %shard_map.114 = (f32[2,48,4,256]{3,2,1,0:T(4,128)}, f32[4,4]{1,0:T(4,128)}) custom-call(f32[2,48,4,256]{3,2,1,0:T(4,128)} %get-tuple-element.4.out_in, f32[4,4]{1,0:T(4,128)} %get-tuple-element.5.coef_in), custom_call_target="tpu_custom_call" | custom-call | tf_op jit(solution)/shard_map/pallas_call | solution.py:693

commit v6 on v5

--- a/solution.py
+++ b/solution.py
@@ -488,13 +488,11 @@
         fold(0, 2, s * q1)
         fold(0, 3, q1 * q1)
 
-    first_end(0)
-    first_end(1)
+    for t in range(4):
+        first_end(t)
     ag_second(1, 0)
-    first_end(2)
+    reduce_first(0)
     ag_second(1, 1)
-    first_end(3)
-    reduce_first(0)
 
     ag_second(1, 2)
     ag_second(1, 3)
@@ -545,17 +543,23 @@
     for kind in range(2):
         for d in range(3):
             fin_copy(kind, d, energy_of(others[d], g)).wait_recv()
+        for q in range(4):
+            (q1_raw, q0_raw)[kind][:, :, q, :] = (fin_q, fin_s)[kind][q].reshape(2, HALF, CH)
     for q in plane:
         rc_copy(q, q).wait_recv()
     lanes = lax.broadcasted_iota(jnp.int32, (1, 128), 1)
     lines = [jnp.zeros((1, 128), f32)] * 4
+    rests, scales = [], []
     for q in range(4):
         tiles = [red_c[i] for i in range(32) if owned(i) == q]
         alpha2, rest2, beta2 = finish(tiles)
-        out[:, :, q, :] = ((fin_s[q] + rest2 * fin_q[q]) / beta2).reshape(2, HALF, CH)
+        rests.append(rest2)
+        scales.append(1.0 / beta2)
         found = (tiles[0][4:5], tiles[0][5:6], wide(alpha2), wide(beta2))
         lines = [jnp.where(lanes == q, new, old) for new, old in zip(found, lines)]
     coef[...] = jnp.concatenate(lines, axis=0)[:, :4]
+    column = lambda v: jnp.broadcast_to(jnp.concatenate(v, axis=0), (4, CH))[None, None]
+    out[...] = (q0_raw[...] + column(rests) * q1_raw[...]) * column(scales)
 
     for d in range(3):
         x_copy(d, tme).wait_send()

time: 103 us -> 101 us (0.981)
  Pallas kernels: 102 us -> 100 us
    pallas_call x1, Pallas kernels: 100 us -> 98.4 us  [body(): pl.pallas_call(kernel, out_shape=(jax.ShapeDtypeStruct((2, HALF, 4, CH),...]
where the time goes in v6:
time: 101 us
  Pallas kernels  100 us (99%)
    pallas_call x1, Pallas kernels, body(): pl.pallas_call(kernel, out_shape=(jax.ShapeDtypeStruct((2, HALF, 4, CH),...  98.4 us

profile of v6, /device:TPU:1, one launch (start us, length us, event | category | flops | bytes accessed | tf_op | source)
XLA Modules:
  0.0 100.9 jit_solution(9751353803702787586)
XLA Ops:
  0.6 98.4 %shard_map.113 = (f32[2,48,4,256]{3,2,1,0:T(4,128)}, f32[4,4]{1,0:T(4,128)}) custom-call(f32[2,48,4,256]{3,2,1,0:T(4,128)} %q1_raw_hbm.1, f32[2,48,4,256]{3,2,1,0:T(4,128)} %q0_raw_hbm.1, f32[4]{0:T(128)} %beta_in.1, f32[2,4,48]{2,1,0:T(4,128)} %bitcast.11, bf16[2048,48]{1,0:T(8,128)(2,1)} %bitcast.7, s32[32,4,32]{2,1,0:T(4,128)} %bitcast.8, ...), custom_call_target="tpu_custom_call" | custom-call | tf_op jit(solution)/shard_map/pallas_call | solution.py:614
  99.1 1.8 %shard_map.114 = (f32[2,48,4,256]{3,2,1,0:T(4,128)}, f32[4,4]{1,0:T(4,128)}) custom-call(f32[2,48,4,256]{3,2,1,0:T(4,128)} %get-tuple-element.4.out_in, f32[4,4]{1,0:T(4,128)} %get-tuple-element.5.coef_in), custom_call_target="tpu_custom_call" | custom-call | tf_op jit(solution)/shard_map/pallas_call | solution.py:697

commit v7 on v6

--- a/solution.py
+++ b/solution.py
@@ -440,14 +440,14 @@
 
     redv[...] = jnp.zeros_like(redv)
     ag_first(0, tme)
-    for d in range(3):
+    for d in (2, 1, 0):
         x_copy(d, others[d]).wait_recv()
         ag_first(0, others[d])
     for load in loads[2:5]:
         load.wait()
     spread_edges(offset_raw, tile_raw, term_raw, count_raw, meta_in, X, g)
     build(tme)
-    order = [tme] + others
+    order = [tme] + others[::-1]
     for t in order:
         ag_second(0, t)
     loads[5].wait()
@@ -456,7 +456,7 @@
     q1g[tme] = q1_in[e]
     q0g[tme] = q0_in[e]
     pg[tme] = prop_in[e]
-    for d in range(3):
+    for d in (2, 1, 0):
         in_copy(0, d, others[d]).wait_recv()
         build(others[d])
     for t in range(4):

time: 101 us -> 100 us (0.990)
  no operation moved by 1% of the time
where the time goes in v7:
time: 100 us
  Pallas kernels  99.4 us (99%)
    pallas_call x1, Pallas kernels, body(): pl.pallas_call(kernel, out_shape=(jax.ShapeDtypeStruct((2, HALF, 4, CH),...  97.6 us

profile of v7, /device:TPU:1, one launch (start us, length us, event | category | flops | bytes accessed | tf_op | source)
XLA Modules:
  0.0 100.1 jit_solution(5120343280382256606)
XLA Ops:
  0.6 97.6 %shard_map.113 = (f32[2,48,4,256]{3,2,1,0:T(4,128)}, f32[4,4]{1,0:T(4,128)}) custom-call(f32[2,48,4,256]{3,2,1,0:T(4,128)} %q1_raw_hbm.1, f32[2,48,4,256]{3,2,1,0:T(4,128)} %q0_raw_hbm.1, f32[4]{0:T(128)} %beta_in.1, f32[2,4,48]{2,1,0:T(4,128)} %bitcast.11, bf16[2048,48]{1,0:T(8,128)(2,1)} %bitcast.7, s32[32,4,32]{2,1,0:T(4,128)} %bitcast.8, ...), custom_call_target="tpu_custom_call" | custom-call | tf_op jit(solution)/shard_map/pallas_call | solution.py:614
  98.3 1.8 %shard_map.114 = (f32[2,48,4,256]{3,2,1,0:T(4,128)}, f32[4,4]{1,0:T(4,128)}) custom-call(f32[2,48,4,256]{3,2,1,0:T(4,128)} %get-tuple-element.4.out_in, f32[4,4]{1,0:T(4,128)} %get-tuple-element.5.coef_in), custom_call_target="tpu_custom_call" | custom-call | tf_op jit(solution)/shard_map/pallas_call | solution.py:697
